TPU v7x, 32 devices: a whole 2x2x4 slice. The times are simulated.
32 devices in a mesh: lon: 16 (over z, y, x), ch: 2 (over core).
Axes of the slice: x: 2, y: 2, z: 4, core: 2. Of those that a mesh axis runs over, the one named last changes fastest.
Arguments:
- coarse: bfloat16 [16, 4, 64, 1024], P(None, None, 'lon', 'ch'), may hold values from -6 to 6
- up_kernel: bfloat16 [4, 4, 1024, 512], P(None, None, 'ch', 'lon'), may hold values from -0.09375 to 0.09375
- up_bias: float32 [512], replicated, may hold values from -3 to 3
- conv_kernel: bfloat16 [3, 3, 512, 512], P(None, None, 'lon'), may hold values from -0.09375 to 0.09375
- conv_bias: float32 [512], replicated, may hold values from -3 to 3
Outputs:
- fine_out: bfloat16 [32, 4, 128, 512], P('ch', None, 'lon')
All inputs are finite; a program needn't handle non-finite values.
Results may differ from a plain program's by a relative error of at most 0.015.
Values may be sent and summed in bfloat16 or wider, within the bound.
No kernel may reach another device: no remote copies, remote signals or barrier semaphores. Data moves between devices by JAX's collectives and lax.ppermute only.
A program may use at most 64 MiB of HBM per device.

v0:
```python
import jax
import jax.numpy as jnp
from jax import lax
from jax.sharding import PartitionSpec as P

TAPS = (((1, 1), (3, 0)), ((2, 1), (0, 2)))


def padded_2(block, sides, width, periodic):
    for axis, dim in sides:
        count = lax.axis_size(axis)
        forward = [(i, i + 1) for i in range(count - 1)]
        if periodic:
            forward.append((count - 1, 0))
        backward = [(target, source) for source, target in forward]
        low = lax.ppermute(
            lax.slice_in_dim(block, block.shape[dim] - width, None, axis=dim), axis, forward
        )
        high = lax.ppermute(lax.slice_in_dim(block, 0, width, axis=dim), axis, backward)
        block = jnp.concatenate([low, block, high], axis=dim)
    return block


def tap_dot(piece, weight):
    return jnp.einsum("rbjc,cn->rbjn", piece, weight, preferred_element_type=jnp.float32)


def upsample(padded, lon_count, weights):
    rows = padded.shape[0] - 2
    batch = padded.shape[1]
    phases = []
    for p in range(2):
        columns = []
        for q in range(2):
            total = None
            for a, row_off in TAPS[p]:
                for c, col_off in TAPS[q]:
                    piece = padded[row_off : row_off + rows, :, col_off : col_off + lon_count, :]
                    term = tap_dot(piece, weights[a, c])
                    total = term if total is None else total + term
            columns.append(total)
        phases.append(jnp.stack(columns, axis=3))
    stacked = jnp.stack(phases, axis=1)
    return stacked.reshape(2 * rows, batch, 2 * lon_count, weights.shape[-1])


def shards(coarse, up_kernel, up_bias, conv_kernel, conv_bias):
    lon_dev = coarse.shape[2]
    row_padded = jnp.pad(coarse, ((1, 1), (0, 0), (0, 0), (0, 0)))
    source = padded_2(row_padded, (("lon", 2),), 1, True)
    up_full = lax.all_gather(up_kernel, "lon", axis=3, tiled=True)
    partial_value = upsample(source, lon_dev, up_full)
    summed = lax.psum_scatter(
        partial_value.astype(jnp.bfloat16), "ch", scatter_dimension=0, tiled=True
    ).astype(jnp.float32)
    hidden = jax.nn.gelu(summed + up_bias, approximate=False).astype(jnp.bfloat16)
    widened = padded_2(hidden, (("lon", 2),), 1, True)
    framed = padded_2(widened, (("ch", 0),), 1, False)
    weights = lax.all_gather(conv_kernel, "lon", axis=2, tiled=True)
    band_rows = hidden.shape[0]
    fine_cols = hidden.shape[2]
    result = jnp.zeros(hidden.shape, jnp.float32) + conv_bias
    for d in range(3):
        for t in range(3):
            result = result + tap_dot(
                framed[d : d + band_rows, :, t : t + fine_cols, :], weights[d, t]
            )
    return result.astype(jnp.bfloat16)


def solution(mesh):
    return jax.shard_map(
        shards,
        mesh=mesh,
        in_specs=(
            P(None, None, "lon", "ch"),
            P(None, None, "ch", "lon"),
            P(),
            P(None, None, "lon", None),
            P(),
        ),
        out_specs=P("ch", None, "lon", None),
        check_vma=False,
    )
```

profile of v0, /device:TPU:0, one launch (start us, length us, event | category | flops | bytes accessed | tf_op | source)
XLA Modules:
  0.0 325.7 jit_solution(8536773265785552722)
XLA Ops:
  6.5 2.2 copy.20
  10.7 2.9 collective-permute-start
  13.6 4.0 %collective-permute-start.1 = (bf16[18,4,1,512]{3,0,2,1:T(8,128)(2,1)}, bf16[18,4,1,512]{3,0,2,1:T(8,128)(2,1)}, u32[]{:S(2)}, u32[]{:S(2)}) collective-permute-start(bf16[18,4,1,512]{3,0,2,1:T(8,128)(2,1)} %get-tuple-element.28), channel_id=1, source_target_pairs={{2,0},{4,2},{6,4},{8,6},{10,8},{12,10},{14,12},{16,14},{18,16},{20... | collective-permute-start | bytes 221192 | tf_op jit(solution)/shard_map/ppermute | solution.py:19
  17.7 108.0 %all-gather.3.cloned.1.call-done = bf16[4,4,512,512]{2,1,0,3:T(4,128)(2,1)} async-done(((bf16[4,4,512,32]{2,1,0,3:T(4,128)(2,1)}), bf16[4,4,512,512]{2,1,0,3:T(4,128)(2,1)}) %all-gather.3.cloned.1.call-update) | async-done | bytes 8388624 | tf_op jit(solution)/shard_map/all_gather | solution.py:51
  125.7 23.2 %fusion.98 = (bf16[1,1,512,512]{2,1,0,3:T(2,128)(2,1)}, bf16[1,1,512,512]{2,1,0,3:T(2,128)(2,1)}, bf16[1,1,512,512]{2,1,0,3:T(2,128)(2,1)}, bf16[1,1,512,512]{2,...) fusion(bf16[4,4,512,512]{2,1,0,3:T(4,128)(2,1)} %all-gather.3.c, ...), kind=kLoop, calls=%fused_computation.146 | loop fusion | bytes 16777216 | tf_op jit(solution)/shard_map/slice | solution.py:39
  148.9 2.3 copy.77
  152.4 2.3 copy.81
  155.8 2.3 copy.69
  159.3 2.3 copy.78
  161.6 3.5 %copy.79 = bf16[1,1,512,512]{3,2,1,0:T(8,128)(2,1)} copy(bf16[1,1,512,512]{2,1,0,3:T(2,128)(2,1)} %get-tuple-element.10) | data formatting | bytes 1048576
  165.1 3.5 %copy.73 = bf16[1,1,512,512]{3,2,1,0:T(8,128)(2,1)} copy(bf16[1,1,512,512]{2,1,0,3:T(2,128)(2,1)} %get-tuple-element.16) | data formatting | bytes 1048576
  168.6 1.5 convolution_add_fusion.7
  171.6 3.5 %copy.80 = bf16[1,1,512,512]{3,2,1,0:T(8,128)(2,1)} copy(bf16[1,1,512,512]{2,1,0,3:T(2,128)(2,1)} %get-tuple-element.9) | data formatting | bytes 1048576
  175.1 3.5 %copy.82 = bf16[1,1,512,512]{3,2,1,0:T(8,128)(2,1)} copy(bf16[1,1,512,512]{2,1,0,3:T(2,128)(2,1)} %get-tuple-element.7) | data formatting | bytes 1048576
  178.6 3.5 %copy.83 = bf16[1,1,512,512]{3,2,1,0:T(8,128)(2,1)} copy(bf16[1,1,512,512]{2,1,0,3:T(2,128)(2,1)} %get-tuple-element.6) | data formatting | bytes 1048576
  182.1 3.5 %copy.84 = bf16[1,1,512,512]{3,2,1,0:T(8,128)(2,1)} copy(bf16[1,1,512,512]{2,1,0,3:T(2,128)(2,1)} %get-tuple-element.20) | data formatting | bytes 1048576
  185.6 3.5 %copy.70 = bf16[1,1,512,512]{3,2,1,0:T(8,128)(2,1)} copy(bf16[1,1,512,512]{2,1,0,3:T(2,128)(2,1)} %get-tuple-element.18) | data formatting | bytes 1048576
  189.0 3.5 %copy.71 = bf16[1,1,512,512]{3,2,1,0:T(8,128)(2,1)} copy(bf16[1,1,512,512]{2,1,0,3:T(2,128)(2,1)} %get-tuple-element.17) | data formatting | bytes 1048576
  192.5 3.5 %copy.72 = bf16[1,1,512,512]{3,2,1,0:T(8,128)(2,1)} copy(bf16[1,1,512,512]{2,1,0,3:T(2,128)(2,1)} %get-tuple-element.5) | data formatting | bytes 1048576
  196.0 3.5 %copy.74 = bf16[1,1,512,512]{3,2,1,0:T(8,128)(2,1)} copy(bf16[1,1,512,512]{2,1,0,3:T(2,128)(2,1)} %get-tuple-element.15) | data formatting | bytes 1048576
  199.5 2.3 copy.75
  201.8 1.3 copy.76
  203.2 1.6 convolution_add_fusion.4
  216.4 6.1 %reduce-scatter.2.cloned.1.call-done = bf16[16,4,8,512]{3,2,1,0:T(8,128)(2,1)} async-done(((bf16[32,4,8,512]{3,2,1,0:T(8,128)(2,1)}), bf16[16,4,8,512]{3,2,1,0:T(8,128)(2,1)}) %reduce-scatter.2.cloned.1.call-update) | async-done | bytes 524304 | tf_op jit(solution)/shard_map/reduce_scatter | solution.py:53
  222.5 3.4 %fusion.18 = bf16[16,4,8,512]{3,2,1,0:T(8,128)(2,1)S(1)} fusion(bf16[16,4,8,512]{3,2,1,0:T(8,128)(2,1)} %reduce-scatter.2.cloned.1.call-done, f32[512]{0:T(512)S(1)} %copy-done.14), kind=kLoop, calls=%fused_computation.35 | loop fusion | flops 17563648 | bytes 1050624 | tf_op jit(solution)/shard_map/convert_element_type | solution.py:56
  226.1 1.8 collective-permute-start.2
  227.8 3.9 %collective-permute-start.3 = (bf16[16,4,1,512]{3,2,1,0:T(2,128)(2,1)S(1)}, bf16[16,4,1,512]{3,2,1,0:T(2,128)(2,1)S(1)}, u32[]{:S(2)}, u32[]{:S(2)}) collective-permute-start(bf16[16,4,1,512]{3,2,1,0:T(2,128)(2,1)S(1)} %get-tuple-element.26), channel_id=1, source_target_pairs={{2,0},{4,2},{6,4},{8,6},{10,8},{12,10},{14,12},{16,14},{18,16},{20... | collective-permute-start | bytes 196616 | tf_op jit(solution)/shard_map/ppermute | solution.py:19
  231.7 75.8 %all-gather.5.cloned.1.call-done = bf16[3,3,512,512]{3,2,1,0:T(8,128)(2,1)} async-done(((bf16[3,3,32,512]{3,2,1,0:T(8,128)(2,1)}), bf16[3,3,512,512]{3,2,1,0:T(8,128)(2,1)}) %all-gather.5.cloned.1.call-update) | async-done | bytes 4718608 | tf_op jit(solution)/shard_map/all_gather | solution.py:59
  307.5 1.5 fusion.36
  310.4 1.6 collective-permute-start.5
  311.9 1.5 fusion.37
  317.7 1.4 fusion.7
  (75 shorter events, 23.8 us)
Async XLA Ops:
  6.5 119.2 %all-gather.3.cloned.1.call-start = ((), (), s32[]{:S(2)}) async-start(), calls=%async_computation.1 | async-start | bytes 8912896 | tf_op jit(solution)/shard_map/all_gather | solution.py:51
  8.8 213.7 %reduce-scatter.2.cloned.1.call-start = ((), (), s32[]{:S(2)}) async-start(), calls=%async_computation.2 | async-start | bytes 1572864 | tf_op jit(solution)/shard_map/reduce_scatter | solution.py:53
  10.7 158.0 %collective-permute-start = (bf16[18,4,1,512]{3,0,2,1:T(8,128)(2,1)}, bf16[18,4,1,512]{3,0,2,1:T(8,128)(2,1)}, u32[]{:S(2)}, u32[]{:S(2)}) collective-permute-start(bf16[18,4,1,512]{3,0,2,1:T(8,128)(2,1)} %get-tuple-element.27), channel_id=1, source_target_pairs={{0,2},{2,4},{4,6},{6,8},{8,10},{10,12},{12,14},{14,16},{16,18},{18... | collective-permute-start | bytes 221192 | tf_op jit(solution)/shard_map/ppermute | solution.py:16
  13.6 189.5 %collective-permute-start.1 = (bf16[18,4,1,512]{3,0,2,1:T(8,128)(2,1)}, bf16[18,4,1,512]{3,0,2,1:T(8,128)(2,1)}, u32[]{:S(2)}, u32[]{:S(2)}) collective-permute-start(bf16[18,4,1,512]{3,0,2,1:T(8,128)(2,1)} %get-tuple-element.28), channel_id=1, source_target_pairs={{2,0},{4,2},{6,4},{8,6},{10,8},{12,10},{14,12},{16,14},{18,16},{20... | collective-permute-start | bytes 221192 | tf_op jit(solution)/shard_map/ppermute | solution.py:19
  17.7 133.5 %copy-start = (bf16[16,4,4,512]{3,2,1,0:T(4,128)(2,1)S(1)}, bf16[16,4,4,512]{3,2,1,0:T(4,128)(2,1)}, u32[]{:S(2)}) copy-start(bf16[16,4,4,512]{3,2,1,0:T(4,128)(2,1)} %param.5) | copy-start | bytes 786436
  168.6 1.5 copy-start.8
  168.6 1.8 copy-start.9
  201.8 3.0 copy-start.6
  203.1 2.0 copy-start.10
  203.1 2.0 copy-start.12
  204.8 1.7 copy-start.7
  205.2 1.7 copy-start.11
  205.2 1.7 copy-start.13
  206.5 1.6 copy-start.5
  206.8 1.6 copy-start.2
  208.1 1.6 copy-start.3
  208.5 2.5 copy-start.4
  214.3 8.2 %copy-start.14 = (f32[512]{0:T(512)S(1)}, f32[512]{0:T(512)}, u32[]{:S(2)}) copy-start(f32[512]{0:T(512)} %param.7) | copy-start | bytes 6148
  215.6 91.9 %all-gather.5.cloned.1.call-start = ((), (), s32[]{:S(2)}) async-start(), calls=%async_computation.3 | async-start | bytes 5013504 | tf_op jit(solution)/shard_map/all_gather | solution.py:59
  226.1 82.9 %collective-permute-start.2 = (bf16[16,4,1,512]{3,2,1,0:T(2,128)(2,1)S(1)}, bf16[16,4,1,512]{3,2,1,0:T(2,128)(2,1)S(1)}, u32[]{:S(2)}, u32[]{:S(2)}) collective-permute-start(bf16[16,4,1,512]{3,2,1,0:T(2,128)(2,1)S(1)} %get-tuple-element.25), channel_id=1, source_target_pairs={{0,2},{2,4},{4,6},{6,8},{8,10},{10,12},{12,14},{14,16},{16,18},{18... | collective-permute-start | bytes 196616 | tf_op jit(solution)/shard_map/ppermute | solution.py:16
  227.8 81.2 %collective-permute-start.3 = (bf16[16,4,1,512]{3,2,1,0:T(2,128)(2,1)S(1)}, bf16[16,4,1,512]{3,2,1,0:T(2,128)(2,1)S(1)}, u32[]{:S(2)}, u32[]{:S(2)}) collective-permute-start(bf16[16,4,1,512]{3,2,1,0:T(2,128)(2,1)S(1)} %get-tuple-element.26), channel_id=1, source_target_pairs={{2,0},{4,2},{6,4},{8,6},{10,8},{12,10},{14,12},{16,14},{18,16},{20... | collective-permute-start | bytes 196616 | tf_op jit(solution)/shard_map/ppermute | solution.py:19
  309.1 4.4 %collective-permute-start.4 = (bf16[1,4,10,512]{3,2,1,0:T(8,128)(2,1)S(1)}, bf16[1,4,10,512]{3,2,1,0:T(8,128)(2,1)S(1)}, u32[]{:S(2)}, u32[]{:S(2)}) collective-permute-start(bf16[1,4,10,512]{3,2,1,0:T(8,128)(2,1)S(1)} %get-tuple-element.23), channel_id=1, source_target_pairs={{0,1},{2,3},{4,5},{6,7},{8,9},{10,11},{12,13},{14,15},{16,17},{18,... | collective-permute-start | bytes 122888 | tf_op jit(solution)/shard_map/ppermute | solution.py:16
  310.4 4.5 %copy-start.1 = (bf16[3,3,512,512]{3,2,1,0:T(8,128)(2,1)S(1)}, bf16[3,3,512,512]{3,2,1,0:T(8,128)(2,1)}, u32[]{:S(2)}) copy-start(bf16[3,3,512,512]{3,2,1,0:T(8,128)(2,1)} %all-gather.5.cloned.1.call-done) | copy-start | bytes 14155780
  310.4 3.4 %collective-permute-start.5 = (bf16[1,4,10,512]{3,2,1,0:T(8,128)(2,1)S(1)}, bf16[1,4,10,512]{3,2,1,0:T(8,128)(2,1)S(1)}, u32[]{:S(2)}, u32[]{:S(2)}) collective-permute-start(bf16[1,4,10,512]{3,2,1,0:T(8,128)(2,1)S(1)} %get-tuple-element.24), channel_id=1, source_target_pairs={{1,0},{3,2},{5,4},{7,6},{9,8},{11,10},{13,12},{15,14},{17,16},{19,... | collective-permute-start | bytes 122888 | tf_op jit(solution)/shard_map/ppermute | solution.py:19
  316.2 0.9 copy-start.15
Sparse Core Ops, SparseCore 0:
  10.1 115.5 all-gather.2
  215.7 6.7 reduce-scatter.1
  225.6 81.8 all-gather.4
where the time goes:
time: 327 us; the launch traced here: 326 us
  waiting for transfers between devices  191 us (58%)
  local copies, waits for them, and re-layouts  77.6 us (24%)
  matrix products  23.3 us (7%)
  starting transfers between devices  15.7 us (5%)
  between operations  13.6 us (4%)
  other arithmetic  4.73 us (1%)
    all_gather x1, waiting for transfers between devices, shards(): up_full = lax.all_gather(up_kernel, 'lon', axis=3, tiled=True)  108 us
    all_gather x1, waiting for transfers between devices, shards(): weights = lax.all_gather(conv_kernel, 'lon', axis=2, tiled=True)  75.8 us
    unnamed x50, local copies, waits for them, and re-layouts  51.3 us
    dot_general x25, matrix products, tap_dot(): jnp.einsum('rbjc,cn->rbjn', piece, weight, preferred_element_type=jnp.flo...  23.3 us
    slice x1, local copies, waits for them, and re-layouts, upsample(): term = tap_dot(piece, weights[a, c])  23.2 us
    ppermute x3, starting transfers between devices, padded_2(): lax.ppermute(lax.slice_in_dim(block, 0, width, axis=dim), axis, backward)  9.46 us
  transfers between devices with their start and end apart: 9, of which 4 were waited for; matrix products, arithmetic and copies ran while one was open for 26% of the time, Pallas kernels for 0%

commit v1 on v0

--- a/solution.py
+++ b/solution.py
@@ -1,9 +1,18 @@
+import functools
+
 import jax
 import jax.numpy as jnp
 from jax import lax
+from jax.experimental import pallas as pl
+from jax.experimental.pallas import tpu as pltpu
 from jax.sharding import PartitionSpec as P
 
 TAPS = (((1, 1), (3, 0)), ((2, 1), (0, 2)))
+FRAME_COST = 0
+PACK_COST = 0
+SPLIT = 12
+VMEM_LIMIT = 16 * 1024 * 1024
+X, Y, Z0, Z1 = 1, 2, 4, 8
 
 
 def padded_2(block, sides, width, periodic):
@@ -44,7 +53,7 @@
     return stacked.reshape(2 * rows, batch, 2 * lon_count, weights.shape[-1])
 
 
-def shards(coarse, up_kernel, up_bias, conv_kernel, conv_bias):
+def general_shards(coarse, up_kernel, up_bias, conv_kernel, conv_bias):
     lon_dev = coarse.shape[2]
     row_padded = jnp.pad(coarse, ((1, 1), (0, 0), (0, 0), (0, 0)))
     source = padded_2(row_padded, (("lon", 2),), 1, True)
@@ -68,7 +77,331 @@
     return result.astype(jnp.bfloat16)
 
 
+def slot_of(lon):
+    return (lon // Y) % 4
+
+
+def group_of(lon):
+    return lon % 2 + 2 * (lon // Z1)
+
+
+def exchange(block, bits):
+    return lax.ppermute(block, "lon", [(i, i ^ bits) for i in range(lax.axis_size("lon"))])
+
+
+def swap_cores(block):
+    return lax.ppermute(block, "ch", [(0, 1), (1, 0)])
+
+
+def pack_body(place, *refs):
+    packed = refs[3]
+    width = refs[0].shape[1]
+    group = 4 * width
+    slot = slot_of(place[1])
+    for j, taps in enumerate(refs[:3]):
+        offset = pl.multiple_of(jnp.bitwise_xor(slot, j) * width, width)
+        for a in range(4):
+            for c in range(4):
+                row = (2 * (a % 2) + c % 2) * group + offset
+                packed[1 - a // 2, 1 - c // 2, pl.ds(row, width), :] = taps[4 * a + c]
+
+
+def pack_last_body(place, first, second, begun, packed):
+    width = first.shape[1]
+    group = 4 * width
+    offset = pl.multiple_of(jnp.bitwise_xor(slot_of(place[1]), 3) * width, width)
+    for a in range(4):
+        for c in range(4):
+            tap = 4 * a + c
+            block = first[tap] if tap < SPLIT else second[tap - SPLIT]
+            row = (2 * (a % 2) + c % 2) * group + offset
+            packed[1 - a // 2, 1 - c // 2, pl.ds(row, width), :] = block
+
+
+def up_body(geo, place, *refs):
+    rows, batch, own = geo
+    pairs, halos, packed, out_ref = (refs[0:2], refs[2:4]), refs[4:6], refs[6], refs[7]
+    low, high = refs[8:]
+    side, right = place[0] if own else 1 - place[0], place[1] % 2
+    band = rows // 2
+    edge = jnp.zeros(low.shape[2:], low.dtype)
+    spare = jnp.zeros((batch, low.shape[3]), low.dtype)
+
+    @pl.loop(0, band + 2)
+    def _(n):
+        row = side * band + n - 1
+        inside = jnp.logical_and(row >= 0, row < rows)
+
+        @pl.when(inside)
+        def _():
+            for s, (mine, partner) in enumerate(pairs):
+                a, b, c, d = halos[s][0, row], mine[row], partner[row], halos[s][1, row]
+                line = jnp.where(
+                    right == 0,
+                    jnp.concatenate([a, b, c, d], axis=0),
+                    jnp.concatenate([d, c, b, a], axis=0),
+                )
+                low[s, n] = line
+                high[s, n] = jnp.concatenate([line[batch:], spare], axis=0)
+
+        @pl.when(jnp.logical_not(inside))
+        def _():
+            for s in range(2):
+                low[s, n] = edge
+                high[s, n] = edge
+
+    for s in range(2):
+        total = None
+        for dy in range(2):
+            for dx, shifted in enumerate((low, high)):
+                left = shifted[s, dy : dy + band + 1].reshape(-1, low.shape[3])
+                term = lax.dot_general(
+                    left, packed[dy, dx], (((1,), (1,)), ((), ())), preferred_element_type=jnp.float32
+                )
+                total = term if total is None else total + term
+        out_ref[s] = total.reshape(out_ref.shape[1:]).astype(out_ref.dtype)
+
+
+def hidden_body(batch, place, *refs):
+    owns, others, bias_ref, outs = refs[0], refs[1], refs[2], refs[3:]
+    core, right = place[0], place[1] % 2
+    cell = outs[0].shape[1]
+    half = outs[0].shape[2] // 2
+    last = outs[0].shape[0] - 1
+    shift = cell - batch
+
+    @pl.loop(0, last + 1)
+    def _(i):
+        for s in range(2):
+            v = owns[s, i].astype(jnp.float32) + others[s, i].astype(jnp.float32) + bias_ref[...]
+            h = v * (1.0 + lax.erf(v * 0.7071067811865476)) * 0.5
+            h = h.astype(jnp.bfloat16)
+            first, second = h[:cell], h[shift : shift + cell]
+            outs[2 * s][i] = jnp.where(right == 0, first, second)
+            outs[2 * s + 1][i] = jnp.where(right == 0, second, first)
+
+    for out in outs:
+
+        @pl.when(core == 0)
+        def _():
+            out[0, :, 0:half] = jnp.zeros((cell, half), jnp.bfloat16)
+
+        @pl.when(core == 1)
+        def _():
+            out[last, :, half:] = jnp.zeros((cell, half), jnp.bfloat16)
+
+
+def frame_body(geo, place, *refs):
+    batch, hops = geo
+    pieces, shifted = refs[: len(hops)], refs[len(hops)]
+    span = shifted.shape[2]
+    group = pieces[0].shape[2] // 4
+    for piece, bits in zip(pieces, hops):
+        source = jnp.bitwise_xor(place[1], bits)
+        offset = pl.multiple_of(group_of(source) * group, group)
+        for i in range(piece.shape[0]):
+            for p in range(2):
+                for q in range(2):
+                    lane = (2 * p + q) * group
+                    block = piece[i, :, lane : lane + group]
+                    shifted[2 * i + p, q, :, pl.ds(offset, group)] = block[0:span]
+                    shifted[2 * i + p, 2 + q, :, pl.ds(offset, group)] = block[batch : batch + span]
+
+
+def conv_body(geo, place, *refs):
+    batch, blocks = geo
+    shifted, mine, others = refs[0], refs[1 : 1 + len(blocks)], refs[1 + len(blocks) : 1 + 2 * len(blocks)]
+    bias_ref, out_ref, packed, total_ref, natural = refs[1 + 2 * len(blocks) :]
+    core, me = place[0], place[1]
+    rows, _, fine, cout = out_ref.shape
+    cols = fine // 2
+    span = cols * batch
+    width = mine[0].shape[2]
+    group = 4 * width
+    half = mine[0].shape[-1]
+    for sources, side in ((mine, core), (others, 1 - core)):
+        lanes = pl.ds(pl.multiple_of(side * half, half), half)
+        for ref, owners in zip(sources, blocks):
+            for n, bits in enumerate(owners):
+                source = jnp.bitwise_xor(me, bits)
+                start = group_of(source) * group + slot_of(source) * width
+                start = pl.multiple_of(start, width)
+                for tap in range(9):
+                    packed[tap, pl.ds(start, width), lanes] = ref[n, tap]
+    total = None
+    for d in range(3):
+        for t in range(3):
+            left = shifted[d : d + rows, t : t + 2].reshape(rows * 2 * span, -1)
+            term = jnp.dot(left, packed[3 * d + t], preferred_element_type=jnp.float32)
+            total = term if total is None else total + term
+    total = (total + bias_ref[...]).reshape(rows, 2, span, -1)
+    for n in range(total_ref.shape[0]):
+        lanes = slice(n * 128, (n + 1) * 128)
+        total_ref[n] = total[..., lanes]
+        for r in range(rows):
+            for c in range(2):
+                for b in range(batch):
+                    natural[n, r, b, pl.ds(c, cols, stride=2), :] = total_ref[
+                        n, r, c, pl.ds(b, cols, stride=batch), :
+                    ]
+        out_ref[:, :, :, lanes] = natural[n].astype(out_ref.dtype)
+
+
+def local_call(body, outs, scratch, flops, *args, aliases={}):
+    specs = [pl.BlockSpec(memory_space=pltpu.SMEM)]
+    specs += [pl.BlockSpec(memory_space=pltpu.VMEM)] * (len(args) - 1)
+    return pl.pallas_call(
+        body,
+        out_shape=outs,
+        in_specs=specs,
+        out_specs=[pl.BlockSpec(memory_space=pltpu.VMEM)] * len(outs),
+        scratch_shapes=scratch,
+        input_output_aliases=aliases,
+        compiler_params=pltpu.CompilerParams(vmem_limit_bytes=VMEM_LIMIT),
+        cost_estimate=pl.CostEstimate(flops=flops, bytes_accessed=8 << 20, transcendentals=0),
+    )(*args)
+
+
+def grouped_shards(coarse, up_kernel, up_bias, conv_kernel, conv_bias):
+    rows, batch, cols, depth = coarse.shape
+    width = up_kernel.shape[3]
+    cout = conv_kernel.shape[3]
+    group = 4 * width
+    half = cout // 2
+    band = rows // 2
+    line = 2 * (cols + 1) * batch
+    cell = (cols + 1) * batch
+    core, me, lon = lax.axis_index("ch"), lax.axis_index("lon"), lax.axis_size("lon")
+    place = jnp.stack([core, me]).astype(jnp.int32)
+
+    taps = up_kernel.transpose(0, 1, 3, 2).reshape(16, width, depth)
+    taps_z = exchange(taps, Z0)
+    taps_y = exchange(taps, Y)
+    edge = lax.dynamic_slice_in_dim(coarse, (cols - 1) * (me % 2), 1, 2)
+    halos = [
+        lax.ppermute(
+            edge, "lon", [(i, (i + (step if i % 2 else -step)) % lon) for i in range(lon)]
+        ).reshape(rows, batch, depth)
+        for step in (1, 2)
+    ]
+    piece = coarse.transpose(0, 2, 1, 3).reshape(rows, cols * batch, depth)
+    near = exchange(piece, X)
+    far = exchange(piece, Z1)
+    kernel, _ = lax.optimization_barrier((conv_kernel, halos))
+    part = lax.dynamic_slice_in_dim(kernel.reshape(9, width, cout), core * half, half, 2)
+    part_z = exchange(part, Z1)
+    bias = up_bias.reshape(2, 4, 2, width)
+    bias = lax.dynamic_slice_in_dim(bias, me // Z1, 1, 0)
+    bias = lax.dynamic_slice_in_dim(bias, me % 2, 1, 2)
+    bias = jnp.tile(bias.reshape(1, group), (1, 4))
+    far, near, taps_y, taps_z, bias, place = lax.optimization_barrier(
+        (far, near, taps_y, taps_z, bias, place)
+    )
+    far_near = exchange(far, X)
+    halos = jnp.stack(halos)
+    far_halos = exchange(halos, Z1)
+    packed_shape = jax.ShapeDtypeStruct((2, 2, 4 * group, depth), jnp.bfloat16)
+    (begun,) = local_call(pack_body, [packed_shape], [], PACK_COST, place, taps, taps_y, taps_z)
+    taps_zy = [exchange(taps_z[:SPLIT], Y), exchange(taps_y[SPLIT:], Z0)]
+    two = jnp.stack([part, part_z])
+    two_z = exchange(two, Z0)
+
+    (packed,) = local_call(
+        pack_last_body, [packed_shape], [], 0, place, *taps_zy, begun, aliases={3: 0}
+    )
+    sums = jax.ShapeDtypeStruct((2, band + 1, line, 4 * group), jnp.bfloat16)
+    chunk = jax.ShapeDtypeStruct((band + 1, cell, 4 * group), jnp.bfloat16)
+
+    def up(own, packed):
+        return local_call(
+            functools.partial(up_body, (rows, batch, own)),
+            [sums],
+            [pltpu.VMEM((2, band + 2, line, depth), jnp.bfloat16)] * 2,
+            2 * 2 * (band + 1) * line * 4 * depth * 4 * group,
+            place,
+            far,
+            far_near,
+            piece,
+            near,
+            far_halos,
+            halos,
+            packed,
+        )
+
+    (given,) = up(False, packed)
+    arrived = swap_cores(given)
+    packed, _ = lax.optimization_barrier((packed, given))
+    (kept,) = up(True, packed)
+    far_same, far_across, near_same, near_across = local_call(
+        functools.partial(hidden_body, batch),
+        [chunk] * 4,
+        [],
+        2 * 40 * (band + 1) * line * 4 * group,
+        place,
+        kept,
+        arrived,
+        bias,
+    )
+    four = jnp.concatenate([two, two_z])
+    four_x, four_y, _ = lax.optimization_barrier((exchange(four, X), exchange(four, Y), far_same))
+    low_xy = exchange(four_y[:2], X)
+    high_xy = exchange(four_x[2:], Y)
+    order = (0, Z1, Z0, Z0 | Z1)
+    mine = [four, four_x, four_y, low_xy, high_xy]
+    owners = (
+        order,
+        tuple(m ^ X for m in order),
+        tuple(m ^ Y for m in order),
+        tuple(m ^ X ^ Y for m in order[:2]),
+        tuple(m ^ X ^ Y for m in order[2:]),
+    )
+    others = [swap_cores(block) for block in mine]
+    hops = (0, X, Z1, X | Z1)
+    pieces = [
+        near_same,
+        exchange(near_across, X),
+        exchange(far_same, Z1),
+        exchange(far_across, X | Z1),
+    ]
+    (framed,) = local_call(
+        functools.partial(frame_body, (batch, hops)),
+        [jax.ShapeDtypeStruct((rows + 2, 4, cols * batch, cout), jnp.bfloat16)],
+        [],
+        FRAME_COST,
+        place,
+        *pieces,
+    )
+    (result,) = local_call(
+        functools.partial(conv_body, (batch, owners)),
+        [jax.ShapeDtypeStruct((rows, batch, 2 * cols, cout), jnp.bfloat16)],
+        [
+            pltpu.VMEM((9, cout, cout), jnp.bfloat16),
+            pltpu.VMEM((cout // 128, rows, 2, cols * batch, 128), jnp.float32),
+            pltpu.VMEM((cout // 128, rows, batch, 2 * cols, 128), jnp.float32),
+        ],
+        2 * rows * 2 * cols * batch * 9 * cout * cout,
+        place,
+        framed,
+        *mine,
+        *others,
+        conv_bias.reshape(1, cout),
+    )
+    return result
+
+
 def solution(mesh):
+    lon, ch = mesh.shape["lon"], mesh.shape["ch"]
+
+    def shards(coarse, up_kernel, up_bias, conv_kernel, conv_bias):
+        fits = (
+            ch == 2
+            and lon == 16
+            and 4 * up_kernel.shape[3] == 128
+            and coarse.shape[1] * coarse.shape[2] == 16
+        )
+        plan = grouped_shards if fits else general_shards
+        return plan(coarse, up_kernel, up_bias, conv_kernel, conv_bias)
+
     return jax.shard_map(
         shards,
         mesh=mesh,

time: 327 us -> 84.9 us (0.26)
  waiting for transfers between devices: 191 us -> 37.6 us
  local copies, waits for them, and re-layouts: 77.6 us -> 3.25 us
  matrix products: 23.3 us -> 0 us
  starting transfers between devices: 15.7 us -> 30 us
  between operations: 13.6 us -> 0.26 us
  Pallas kernels: 0 us -> 13.3 us
  other arithmetic: 4.73 us -> 0.25 us
    all_gather x2 -> x0, waiting for transfers between devices: 184 us -> none  [the longest x1 108 us: shards(): up_full = lax.all_gather(up_kernel, 'lon', axis=3, tiled=True)]
    unnamed x50 -> x7, local copies, waits for them, and re-layouts: 51.3 us -> 0.05 us
    ppermute x6 -> x25, waiting for transfers between devices: 0.36 us -> 37.6 us  [the longest x17 36.9 us: exchange(): lax.ppermute(block, 'lon', [(i, i ^ bits) for i in range(lax.axis_size('l...]
    slice x3 -> x4, local copies, waits for them, and re-layouts: 24.1 us -> 0.08 us  [the longest x2 0.04 us: grouped_shards(): taps_zy = [exchange(taps_z[:SPLIT], Y), exchange(taps_y[SPLIT:], Z0)]]
    dot_general x25 -> x0, matrix products: 23.3 us -> none  [tap_dot(): jnp.einsum('rbjc,cn->rbjn', piece, weight, preferred_element_type=jnp.flo...]
    ppermute x6 -> x25, starting transfers between devices: 15.5 us -> 30 us  [the longest x17 27.6 us: exchange(): lax.ppermute(block, 'lon', [(i, i ^ bits) for i in range(lax.axis_size('l...]
    pallas_call x0 -> x7, Pallas kernels: none -> 13.3 us  [local_call(): pl.pallas_call(body, out_shape=outs, in_specs=specs, out_specs=[pl.BlockS...]
    reduce_scatter x1 -> x0, waiting for transfers between devices: 6.13 us -> none  [shards(): lax.psum_scatter(partial_value.astype(jnp.bfloat16), 'ch', scatter_dimens...]
  transfers between devices with their start and end apart: 9 -> 25, of which waited for: 4 -> 11; matrix products, arithmetic and copies ran while one was open for 26% -> 4% of each run, Pallas kernels for 0% -> 10%
where the time goes in v1:
time: 84.9 us; the launch traced here: 84.7 us
  waiting for transfers between devices  37.6 us (44%)
  starting transfers between devices  30 us (35%)
  Pallas kernels  13.3 us (16%)
  local copies, waits for them, and re-layouts  3.25 us (4%)
    ppermute x17, waiting for transfers between devices, exchange(): lax.ppermute(block, 'lon', [(i, i ^ bits) for i in range(lax.axis_size('l...  36.9 us
    ppermute x17, starting transfers between devices, exchange(): lax.ppermute(block, 'lon', [(i, i ^ bits) for i in range(lax.axis_size('l...  27.6 us
    pallas_call x7, Pallas kernels, local_call(): pl.pallas_call(body, out_shape=outs, in_specs=specs, out_specs=[pl.BlockS...  13.3 us
    ppermute x2, starting transfers between devices, grouped_shards(): lax.ppermute(edge, 'lon', [(i, (i + (step if i % 2 else -step)) % lon) fo...  1.78 us
  transfers between devices with their start and end apart: 25, of which 11 were waited for; matrix products, arithmetic and copies ran while one was open for 4% of the time, Pallas kernels for 10%

profile of v1, /device:TPU:0, one launch (start us, length us, event | category | flops | bytes accessed | tf_op | source)
XLA Modules:
  0.0 84.7 jit_solution(17376922554057752254)
XLA Ops:
  0.0 3.0 %collective-permute-start.2 = (bf16[16,32,512]{2,1,0:T(8,128)(2,1)}, bf16[16,32,512]{2,1,0:T(8,128)(2,1)S(1)}, u32[]{:S(2)}, u32[]{:S(2)}) collective-permute-start(bf16[16,32,512]{2,1,0:T(8,128)(2,1)} %bitcast.16), channel_id=1, source_target_pairs={{0,4},{2,6},{4,0},{6,2},{8,12},{10,14},{12,8},{14,10},{16,20},{18,... | collective-permute-start | bytes 1572872 | tf_op jit(solution)/shard_map/ppermute | solution.py:89
  3.0 1.6 %collective-permute-start.3 = (bf16[16,32,512]{2,1,0:T(8,128)(2,1)}, bf16[16,32,512]{2,1,0:T(8,128)(2,1)S(1)}, u32[]{:S(2)}, u32[]{:S(2)}) collective-permute-start(bf16[16,32,512]{2,1,0:T(8,128)(2,1)} %bitcast.17), channel_id=1, source_target_pairs={{0,8},{2,10},{4,12},{6,14},{8,0},{10,2},{12,4},{14,6},{16,24},{18,... | collective-permute-start | bytes 1572872 | tf_op jit(solution)/shard_map/ppermute | solution.py:89
  4.5 1.1 %copy.9 = bf16[16,4,4,512]{3,2,1,0:T(4,128)(2,1)S(1)} copy(bf16[16,4,4,512]{3,1,2,0:T(4,128)(2,1)} %bitcast.23) | data formatting | bytes 524288 | tf_op jit(solution)/shard_map/transpose | solution.py:287
  5.7 2.7 %collective-permute-start = (bf16[16,16,512]{2,1,0:T(8,128)(2,1)S(1)}, bf16[16,16,512]{2,1,0:T(8,128)(2,1)S(1)}, u32[]{:S(2)}, u32[]{:S(2)}) collective-permute-start(bf16[16,16,512]{2,1,0:T(8,128)(2,1)S(1)} %reshape.23.refs_2_), channel_id=1, source_target_pairs={{0,16},{2,18},{4,20},{6,22},{8,24},{10,26},{12,28},{14,30},{16,0},... | collective-permute-start | bytes 786440 | tf_op jit(solution)/shard_map/ppermute | solution.py:89
  8.4 1.5 %collective-permute-start.1 = (bf16[16,16,512]{2,1,0:T(8,128)(2,1)S(1)}, bf16[16,16,512]{2,1,0:T(8,128)(2,1)S(1)}, u32[]{:S(2)}, u32[]{:S(2)}) collective-permute-start(bf16[16,16,512]{2,1,0:T(8,128)(2,1)S(1)} %reshape.23.refs_2_), channel_id=1, source_target_pairs={{0,2},{2,0},{4,6},{6,4},{8,10},{10,8},{12,14},{14,12},{16,18},{18,... | collective-permute-start | bytes 786440 | tf_op jit(solution)/shard_map/ppermute | solution.py:89
  9.8 1.1 %constant_dynamic-slice_fusion.1 = bf16[16,4,1,512]{3,2,1,0:T(2,128)(2,1)S(1)} fusion(bf16[16,4,4,512]{3,2,1,0:T(4,128)(2,1)} %param.5, s32[]{:T(128)S(6)} %select_n.35), kind=kLoop, calls=%fused_computation.5 | loop fusion | bytes 131076 | tf_op jit(solution)/shard_map/dynamic_slice | solution.py:280
  11.1 0.8 reshape.25
  12.0 9.9 %collective-permute-done.refs_0_ = bf16[16,16,512]{2,1,0:T(8,128)(2,1)S(1)} collective-permute-done((bf16[16,16,512]{2,1,0:T(8,128)(2,1)S(1)}, bf16[16,16,512]{2,1,0:T(8,128)(2,1)S(1)}, u32[]{:S(2)}, u32[]{:S(2)}) %collective-permute-start) | collective-permute-done | bytes 262176 | tf_op jit(solution)/shard_map/ppermute | solution.py:89
  22.0 1.7 %collective-permute-start.6 = (bf16[16,4,1,512]{3,1,0,2:T(4,128)(2,1)S(1)}, bf16[16,4,1,512]{3,1,0,2:T(4,128)(2,1)S(1)}, u32[]{:S(2)}, u32[]{:S(2)}) collective-permute-start(bf16[16,4,1,512]{3,1,0,2:T(4,128)(2,1)S(1)} %copy.11), channel_id=1, source_target_pairs={{0,28},{2,6},{4,0},{6,10},{8,4},{10,14},{12,8},{14,18},{16,12},{18... | collective-permute-start | bytes 196616 | tf_op jit(solution)/shard_map/ppermute | solution.py:282
  24.1 3.4 %collective-permute-start.14 = (bf16[9,32,256]{2,1,0:T(8,128)(2,1)S(1)}, bf16[9,32,256]{2,1,0:T(8,128)(2,1)S(1)}, u32[]{:S(2)}, u32[]{:S(2)}) collective-permute-start(bf16[9,32,256]{2,1,0:T(8,128)(2,1)S(1)} %constant_dynamic-slice_fusion), channel_id=1, source_target_pairs={{0,16},{2,18},{4,20},{6,22},{8,24},{10,26},{12,28},{14,30},{16,0},... | collective-permute-start | bytes 442376 | tf_op jit(solution)/shard_map/ppermute | solution.py:89
  28.1 2.9 %collective-permute-start.7 = (bf16[2,16,4,512]{3,2,1,0:T(4,128)(2,1)S(1)}, bf16[2,16,4,512]{3,2,1,0:T(4,128)(2,1)S(1)}, u32[]{:S(2)}, u32[]{:S(2)}) collective-permute-start(bf16[2,16,4,512]{3,2,1,0:T(4,128)(2,1)S(1)} %pad_maximum_fusion.2.refs_5_), channel_id=1, source_target_pairs={{0,16},{2,18},{4,20},{6,22},{8,24},{10,26},{12,28},{14,30},{16,0},... | collective-permute-start | bytes 393224 | tf_op jit(solution)/shard_map/ppermute | solution.py:89
  31.0 0.5 collective-permute-start.9
  31.6 5.5 %collective-permute-done.14 = bf16[9,32,256]{2,1,0:T(8,128)(2,1)S(1)} collective-permute-done((bf16[9,32,256]{2,1,0:T(8,128)(2,1)S(1)}, bf16[9,32,256]{2,1,0:T(8,128)(2,1)S(1)}, u32[]{:S(2)}, u32[]{:S(2)}) %collective-permute-start.14) | collective-permute-done | bytes 147488 | tf_op jit(solution)/shard_map/ppermute | solution.py:89
  37.2 0.7 shard_map.55.begun
  37.9 2.3 %collective-permute-done.9.second = bf16[4,32,512]{2,1,0:T(8,128)(2,1)S(1)} collective-permute-done((bf16[4,32,512]{2,1,0:T(8,128)(2,1)S(1)}, bf16[4,32,512]{2,1,0:T(8,128)(2,1)S(1)}, u32[]{:S(2)}, u32[]{:S(2)}) %collective-permute-start.9) | collective-permute-done | bytes 131104 | tf_op jit(solution)/shard_map/ppermute | solution.py:89
  40.2 0.6 shard_map.56.refs_6_
  40.8 2.7 %shard_map.57 = bf16[2,9,40,512]{3,2,1,0:T(8,128)(2,1)S(1)} custom-call(s32[2]{0:T(128)S(1)} %pad_add_fusion.place, bf16[16,16,512]{2,1,0:T(8,128)(2,1)S(1)} %collective-permute-done.refs_0_, bf16[16,16,512]{2,1,0:T(8,128)(2,1)S(1)} %collective-permute-done.4.refs_1_, bf16[16,16,512]{2,1,0:T(8,128)(2,1)S(1)} %reshape.23.refs_2_, ...), custom_call_target="tpu_custom_call" | custom-call | flops 1509949440 | bytes 8388608 | tf_op jit(solution)/shard_map/pallas_call | solution.py:253
  43.6 0.9 %collective-permute-done.15 = bf16[2,9,32,256]{3,2,1,0:T(8,128)(2,1)S(1)} collective-permute-done((bf16[2,9,32,256]{3,2,1,0:T(8,128)(2,1)S(1)}, bf16[2,9,32,256]{3,2,1,0:T(8,128)(2,1)S(1)}, u32[]{:S(2)}, u32[]{:S(2)}) %collective-permute-start.15) | collective-permute-done | bytes 294944 | tf_op jit(solution)/shard_map/ppermute | solution.py:89
  44.5 4.7 %collective-permute-start.16 = (bf16[4,9,32,256]{3,2,1,0:T(8,128)(2,1)S(1)}, bf16[4,9,32,256]{3,2,1,0:T(8,128)(2,1)S(1)}, u32[]{:S(2)}, u32[]{:S(2)}) collective-permute-start(bf16[4,9,32,256]{3,2,1,0:T(8,128)(2,1)S(1)} %pad_maximum_fusion.refs_1_), channel_id=1, source_target_pairs={{0,2},{2,0},{4,6},{6,4},{8,10},{10,8},{12,14},{14,12},{16,18},{18,... | collective-permute-start | bytes 1769480 | tf_op jit(solution)/shard_map/ppermute | solution.py:89
  49.2 2.7 %shard_map.58.refs_0_ = bf16[2,9,40,512]{3,2,1,0:T(8,128)(2,1)S(1)} custom-call(s32[2]{0:T(128)S(1)} %pad_add_fusion.place, bf16[16,16,512]{2,1,0:T(8,128)(2,1)S(1)} %collective-permute-done.refs_0_, bf16[16,16,512]{2,1,0:T(8,128)(2,1)S(1)} %collective-permute-done.4.refs_1_, bf16[16,16,512]{2,1,0:T(8,128)(2,1)S(1)} %reshape.23.refs_2_, ...), custom_call_target="tpu_custom_call" | custom-call | flops 1509949440 | bytes 8388608 | tf_op jit(solution)/shard_map/pallas_call | solution.py:253
  51.9 1.2 %shard_map.59 = (bf16[9,20,512]{2,1,0:T(8,128)(2,1)S(1)}, bf16[9,20,512]{2,1,0:T(8,128)(2,1)S(1)}, bf16[9,20,512]{2,1,0:T(8,128)(2,1)S(1)}, bf16[9,20,512]{2,1,0:T(8,128)(2,1)S(1)}) custom-call(s32[2]{0:T(128)S(1)} %pad_add_fusion.place, bf16[2,9,40,512]{3,2,1,0:T(8,128)(2,1)S(1)} %shard_map.58.refs_0_, ...), custom_call_target="tpu_custom_call" | custom-call | flops 14745600 | bytes 8388608 | tf_op jit(solution)/shard_map/pallas_call | solution.py:253
  53.3 0.7 collective-permute-start.12
  54.0 3.6 %collective-permute-start.13 = (bf16[9,20,512]{2,1,0:T(8,128)(2,1)S(1)}, bf16[9,20,512]{2,1,0:T(8,128)(2,1)S(1)}, u32[]{:S(2)}, u32[]{:S(2)}) collective-permute-start(bf16[9,20,512]{2,1,0:T(8,128)(2,1)S(1)} %get-tuple-element.28), channel_id=1, source_target_pairs={{0,18},{2,16},{4,22},{6,20},{8,26},{10,24},{12,30},{14,28},{16,2},... | collective-permute-start | bytes 552968 | tf_op jit(solution)/shard_map/ppermute | solution.py:89
  57.6 5.9 %collective-permute-done.16.refs_2_ = bf16[4,9,32,256]{3,2,1,0:T(8,128)(2,1)S(1)} collective-permute-done((bf16[4,9,32,256]{3,2,1,0:T(8,128)(2,1)S(1)}, bf16[4,9,32,256]{3,2,1,0:T(8,128)(2,1)S(1)}, u32[]{:S(2)}, u32[]{:S(2)}) %collective-permute-start.16) | collective-permute-done | bytes 589856 | tf_op jit(solution)/shard_map/ppermute | solution.py:89
  63.5 2.1 %collective-permute-start.18 = (bf16[2,9,32,256]{3,2,1,0:T(8,128)(2,1)S(1)}, bf16[2,9,32,256]{3,2,1,0:T(8,128)(2,1)S(1)}, u32[]{:S(2)}, u32[]{:S(2)}) collective-permute-start(bf16[2,9,32,256]{3,2,1,0:T(8,128)(2,1)S(1)} %slice.14), channel_id=1, source_target_pairs={{0,2},{2,0},{4,6},{6,4},{8,10},{10,8},{12,14},{14,12},{16,18},{18,... | collective-permute-start | bytes 884744 | tf_op jit(solution)/shard_map/ppermute | solution.py:89
  65.6 0.9 %collective-permute-done.11.refs_1_ = bf16[9,20,512]{2,1,0:T(8,128)(2,1)S(1)} collective-permute-done((bf16[9,20,512]{2,1,0:T(8,128)(2,1)S(1)}, bf16[9,20,512]{2,1,0:T(8,128)(2,1)S(1)}, u32[]{:S(2)}, u32[]{:S(2)}) %collective-permute-start.11) | collective-permute-done | bytes 184352 | tf_op jit(solution)/shard_map/ppermute | solution.py:89
  66.5 3.4 %collective-permute-done.12.refs_2_ = bf16[9,20,512]{2,1,0:T(8,128)(2,1)S(1)} collective-permute-done((bf16[9,20,512]{2,1,0:T(8,128)(2,1)S(1)}, bf16[9,20,512]{2,1,0:T(8,128)(2,1)S(1)}, u32[]{:S(2)}, u32[]{:S(2)}) %collective-permute-start.12) | collective-permute-done | bytes 184352 | tf_op jit(solution)/shard_map/ppermute | solution.py:89
  69.9 5.8 %collective-permute-done.13.refs_3_ = bf16[9,20,512]{2,1,0:T(8,128)(2,1)S(1)} collective-permute-done((bf16[9,20,512]{2,1,0:T(8,128)(2,1)S(1)}, bf16[9,20,512]{2,1,0:T(8,128)(2,1)S(1)}, u32[]{:S(2)}, u32[]{:S(2)}) %collective-permute-start.13) | collective-permute-done | bytes 184352 | tf_op jit(solution)/shard_map/ppermute | solution.py:89
  75.7 2.3 %collective-permute-done.18.refs_4_ = bf16[2,9,32,256]{3,2,1,0:T(8,128)(2,1)S(1)} collective-permute-done((bf16[2,9,32,256]{3,2,1,0:T(8,128)(2,1)S(1)}, bf16[2,9,32,256]{3,2,1,0:T(8,128)(2,1)S(1)}, u32[]{:S(2)}, u32[]{:S(2)}) %collective-permute-start.18) | collective-permute-done | bytes 294944 | tf_op jit(solution)/shard_map/ppermute | solution.py:89
  78.0 0.5 collective-permute-start.24
  78.5 0.8 shard_map.60.refs_0_
  80.0 4.7 %shard_map.61 = bf16[16,4,8,512]{3,2,1,0:T(8,128)(2,1)} custom-call(s32[2]{0:T(128)S(1)} %pad_add_fusion.place, bf16[18,4,16,512]{3,2,1,0:T(8,128)(2,1)S(1)} %shard_map.60.refs_0_, bf16[4,9,32,256]{3,2,1,0:T(8,128)(2,1)S(1)} %pad_maximum_fusion.refs_1_, bf16[4,9,32,256]{3,2,1,0:T(8,128)(2,1)S(1)} %collective-permute-done.16.refs_2_, ...), custom_call_target="tpu_custom_call" | custom-call | flops 2415919104 | bytes 8388608 | tf_op jit(solution)/shard_map/pallas_call | solution.py:253
  (49 shorter events, 2.5 us)
Async XLA Ops:
  0.0 24.1 %copy-start = (bf16[3,3,32,512]{3,2,1,0:T(8,128)(2,1)S(1)}, bf16[3,3,32,512]{3,2,1,0:T(8,128)(2,1)}, u32[]{:S(2)}) copy-start(bf16[3,3,32,512]{3,2,1,0:T(8,128)(2,1)} %param.8) | copy-start | bytes 884740
  0.0 37.2 %copy-start.1 = (bf16[4,4,512,32]{2,3,1,0:T(8,128)(2,1)S(1)}, bf16[4,4,512,32]{2,3,1,0:T(8,128)(2,1)}, u32[]{:S(2)}) copy-start(bf16[4,4,512,32]{2,3,1,0:T(8,128)(2,1)} %param.6) | copy-start | bytes 1572868
  0.0 23.7 %collective-permute-start.2 = (bf16[16,32,512]{2,1,0:T(8,128)(2,1)}, bf16[16,32,512]{2,1,0:T(8,128)(2,1)S(1)}, u32[]{:S(2)}, u32[]{:S(2)}) collective-permute-start(bf16[16,32,512]{2,1,0:T(8,128)(2,1)} %bitcast.16), channel_id=1, source_target_pairs={{0,4},{2,6},{4,0},{6,2},{8,12},{10,14},{12,8},{14,10},{16,20},{18,... | collective-permute-start | bytes 1572872 | tf_op jit(solution)/shard_map/ppermute | solution.py:89
  3.0 20.7 %collective-permute-start.3 = (bf16[16,32,512]{2,1,0:T(8,128)(2,1)}, bf16[16,32,512]{2,1,0:T(8,128)(2,1)S(1)}, u32[]{:S(2)}, u32[]{:S(2)}) collective-permute-start(bf16[16,32,512]{2,1,0:T(8,128)(2,1)} %bitcast.17), channel_id=1, source_target_pairs={{0,8},{2,10},{4,12},{6,14},{8,0},{10,2},{12,4},{14,6},{16,24},{18,... | collective-permute-start | bytes 1572872 | tf_op jit(solution)/shard_map/ppermute | solution.py:89
  5.7 16.3 %collective-permute-start = (bf16[16,16,512]{2,1,0:T(8,128)(2,1)S(1)}, bf16[16,16,512]{2,1,0:T(8,128)(2,1)S(1)}, u32[]{:S(2)}, u32[]{:S(2)}) collective-permute-start(bf16[16,16,512]{2,1,0:T(8,128)(2,1)S(1)} %reshape.23.refs_2_), channel_id=1, source_target_pairs={{0,16},{2,18},{4,20},{6,22},{8,24},{10,26},{12,28},{14,30},{16,0},... | collective-permute-start | bytes 786440 | tf_op jit(solution)/shard_map/ppermute | solution.py:89
  8.4 15.3 %collective-permute-start.1 = (bf16[16,16,512]{2,1,0:T(8,128)(2,1)S(1)}, bf16[16,16,512]{2,1,0:T(8,128)(2,1)S(1)}, u32[]{:S(2)}, u32[]{:S(2)}) collective-permute-start(bf16[16,16,512]{2,1,0:T(8,128)(2,1)S(1)} %reshape.23.refs_2_), channel_id=1, source_target_pairs={{0,2},{2,0},{4,6},{6,4},{8,10},{10,8},{12,14},{14,12},{16,18},{18,... | collective-permute-start | bytes 786440 | tf_op jit(solution)/shard_map/ppermute | solution.py:89
  11.0 17.0 %collective-permute-start.5 = (bf16[16,4,1,512]{3,1,0,2:T(4,128)(2,1)S(1)}, bf16[16,4,1,512]{3,1,0,2:T(4,128)(2,1)S(1)}, u32[]{:S(2)}, u32[]{:S(2)}) collective-permute-start(bf16[16,4,1,512]{3,1,0,2:T(4,128)(2,1)S(1)} %copy.11), channel_id=1, source_target_pairs={{0,30},{2,4},{4,2},{6,8},{8,6},{10,12},{12,10},{14,16},{16,14},{18... | collective-permute-start | bytes 196616 | tf_op jit(solution)/shard_map/ppermute | solution.py:282
  22.0 6.0 %collective-permute-start.6 = (bf16[16,4,1,512]{3,1,0,2:T(4,128)(2,1)S(1)}, bf16[16,4,1,512]{3,1,0,2:T(4,128)(2,1)S(1)}, u32[]{:S(2)}, u32[]{:S(2)}) collective-permute-start(bf16[16,4,1,512]{3,1,0,2:T(4,128)(2,1)S(1)} %copy.11), channel_id=1, source_target_pairs={{0,28},{2,6},{4,0},{6,10},{8,4},{10,14},{12,8},{14,18},{16,12},{18... | collective-permute-start | bytes 196616 | tf_op jit(solution)/shard_map/ppermute | solution.py:282
  23.8 16.4 %collective-permute-start.8 = (bf16[12,32,512]{2,1,0:T(8,128)(2,1)S(1)}, bf16[12,32,512]{2,1,0:T(8,128)(2,1)S(1)}, u32[]{:S(2)}, u32[]{:S(2)}) collective-permute-start(bf16[12,32,512]{2,1,0:T(8,128)(2,1)S(1)} %slice.12), channel_id=1, source_target_pairs={{0,4},{2,6},{4,0},{6,2},{8,12},{10,14},{12,8},{14,10},{16,20},{18,... | collective-permute-start | bytes 1179656 | tf_op jit(solution)/shard_map/ppermute | solution.py:89
  24.1 13.0 %collective-permute-start.14 = (bf16[9,32,256]{2,1,0:T(8,128)(2,1)S(1)}, bf16[9,32,256]{2,1,0:T(8,128)(2,1)S(1)}, u32[]{:S(2)}, u32[]{:S(2)}) collective-permute-start(bf16[9,32,256]{2,1,0:T(8,128)(2,1)S(1)} %constant_dynamic-slice_fusion), channel_id=1, source_target_pairs={{0,16},{2,18},{4,20},{6,22},{8,24},{10,26},{12,28},{14,30},{16,0},... | collective-permute-start | bytes 442376 | tf_op jit(solution)/shard_map/ppermute | solution.py:89
  27.6 13.2 %collective-permute-start.4 = (bf16[16,16,512]{2,1,0:T(8,128)(2,1)S(1)}, bf16[16,16,512]{2,1,0:T(8,128)(2,1)S(1)}, u32[]{:S(2)}, u32[]{:S(2)}) collective-permute-start(bf16[16,16,512]{2,1,0:T(8,128)(2,1)S(1)} %collective-permute-done.refs_0_), channel_id=1, source_target_pairs={{0,2},{2,0},{4,6},{6,4},{8,10},{10,8},{12,14},{14,12},{16,18},{18,... | collective-permute-start | bytes 786440 | tf_op jit(solution)/shard_map/ppermute | solution.py:89
  28.1 12.7 %collective-permute-start.7 = (bf16[2,16,4,512]{3,2,1,0:T(4,128)(2,1)S(1)}, bf16[2,16,4,512]{3,2,1,0:T(4,128)(2,1)S(1)}, u32[]{:S(2)}, u32[]{:S(2)}) collective-permute-start(bf16[2,16,4,512]{3,2,1,0:T(4,128)(2,1)S(1)} %pad_maximum_fusion.2.refs_5_), channel_id=1, source_target_pairs={{0,16},{2,18},{4,20},{6,22},{8,24},{10,26},{12,28},{14,30},{16,0},... | collective-permute-start | bytes 393224 | tf_op jit(solution)/shard_map/ppermute | solution.py:89
  31.0 9.1 %collective-permute-start.9 = (bf16[4,32,512]{2,1,0:T(8,128)(2,1)S(1)}, bf16[4,32,512]{2,1,0:T(8,128)(2,1)S(1)}, u32[]{:S(2)}, u32[]{:S(2)}) collective-permute-start(bf16[4,32,512]{2,1,0:T(8,128)(2,1)S(1)} %slice.13), channel_id=1, source_target_pairs={{0,8},{2,10},{4,12},{6,14},{8,0},{10,2},{12,4},{14,6},{16,24},{18,... | collective-permute-start | bytes 393224 | tf_op jit(solution)/shard_map/ppermute | solution.py:89
  37.1 7.3 %collective-permute-start.15 = (bf16[2,9,32,256]{3,2,1,0:T(8,128)(2,1)S(1)}, bf16[2,9,32,256]{3,2,1,0:T(8,128)(2,1)S(1)}, u32[]{:S(2)}, u32[]{:S(2)}) collective-permute-start(bf16[2,9,32,256]{3,2,1,0:T(8,128)(2,1)S(1)} %pad_maximum_fusion.1), channel_id=1, source_target_pairs={{0,8},{2,10},{4,12},{6,14},{8,0},{10,2},{12,4},{14,6},{16,24},{18,... | collective-permute-start | bytes 884744 | tf_op jit(solution)/shard_map/ppermute | solution.py:89
  43.5 8.4 %collective-permute-start.10 = (bf16[2,9,40,512]{3,2,1,0:T(8,128)(2,1)S(1)}, bf16[2,9,40,512]{3,2,1,0:T(8,128)(2,1)S(1)}, u32[]{:S(2)}, u32[]{:S(2)}) collective-permute-start(bf16[2,9,40,512]{3,2,1,0:T(8,128)(2,1)S(1)} %shard_map.57), channel_id=1, source_target_pairs={{0,1},{1,0},{2,3},{3,2},{4,5},{5,4},{6,7},{7,6},{8,9},{9,8},{10,11... | collective-permute-start | bytes 2211848 | tf_op jit(solution)/shard_map/ppermute | solution.py:93
  44.5 18.9 %collective-permute-start.16 = (bf16[4,9,32,256]{3,2,1,0:T(8,128)(2,1)S(1)}, bf16[4,9,32,256]{3,2,1,0:T(8,128)(2,1)S(1)}, u32[]{:S(2)}, u32[]{:S(2)}) collective-permute-start(bf16[4,9,32,256]{3,2,1,0:T(8,128)(2,1)S(1)} %pad_maximum_fusion.refs_1_), channel_id=1, source_target_pairs={{0,2},{2,0},{4,6},{6,4},{8,10},{10,8},{12,14},{14,12},{16,18},{18,... | collective-permute-start | bytes 1769480 | tf_op jit(solution)/shard_map/ppermute | solution.py:89
  49.2 14.2 %collective-permute-start.17 = (bf16[4,9,32,256]{3,2,1,0:T(8,128)(2,1)S(1)}, bf16[4,9,32,256]{3,2,1,0:T(8,128)(2,1)S(1)}, u32[]{:S(2)}, u32[]{:S(2)}) collective-permute-start(bf16[4,9,32,256]{3,2,1,0:T(8,128)(2,1)S(1)} %pad_maximum_fusion.refs_1_), channel_id=1, source_target_pairs={{0,4},{2,6},{4,0},{6,2},{8,12},{10,14},{12,8},{14,10},{16,20},{18,... | collective-permute-start | bytes 1769480 | tf_op jit(solution)/shard_map/ppermute | solution.py:89
  51.9 28.1 %copy-start.2 = (f32[512]{0:T(512)S(1)}, f32[512]{0:T(512)}, u32[]{:S(2)}) copy-start(f32[512]{0:T(512)} %param.9) | copy-start | bytes 6148
  53.1 13.4 %collective-permute-start.11 = (bf16[9,20,512]{2,1,0:T(8,128)(2,1)S(1)}, bf16[9,20,512]{2,1,0:T(8,128)(2,1)S(1)}, u32[]{:S(2)}, u32[]{:S(2)}) collective-permute-start(bf16[9,20,512]{2,1,0:T(8,128)(2,1)S(1)} %get-tuple-element.26), channel_id=1, source_target_pairs={{0,2},{2,0},{4,6},{6,4},{8,10},{10,8},{12,14},{14,12},{16,18},{18,... | collective-permute-start | bytes 552968 | tf_op jit(solution)/shard_map/ppermute | solution.py:89
  53.3 16.6 %collective-permute-start.12 = (bf16[9,20,512]{2,1,0:T(8,128)(2,1)S(1)}, bf16[9,20,512]{2,1,0:T(8,128)(2,1)S(1)}, u32[]{:S(2)}, u32[]{:S(2)}) collective-permute-start(bf16[9,20,512]{2,1,0:T(8,128)(2,1)S(1)} %get-tuple-element.27), channel_id=1, source_target_pairs={{0,16},{2,18},{4,20},{6,22},{8,24},{10,26},{12,28},{14,30},{16,0},... | collective-permute-start | bytes 552968 | tf_op jit(solution)/shard_map/ppermute | solution.py:89
  54.0 21.7 %collective-permute-start.13 = (bf16[9,20,512]{2,1,0:T(8,128)(2,1)S(1)}, bf16[9,20,512]{2,1,0:T(8,128)(2,1)S(1)}, u32[]{:S(2)}, u32[]{:S(2)}) collective-permute-start(bf16[9,20,512]{2,1,0:T(8,128)(2,1)S(1)} %get-tuple-element.28), channel_id=1, source_target_pairs={{0,18},{2,16},{4,22},{6,20},{8,26},{10,24},{12,30},{14,28},{16,2},... | collective-permute-start | bytes 552968 | tf_op jit(solution)/shard_map/ppermute | solution.py:89
  63.4 15.9 %collective-permute-start.20 = (bf16[4,9,32,256]{3,2,1,0:T(8,128)(2,1)S(1)}, bf16[4,9,32,256]{3,2,1,0:T(8,128)(2,1)S(1)}, u32[]{:S(2)}, u32[]{:S(2)}) collective-permute-start(bf16[4,9,32,256]{3,2,1,0:T(8,128)(2,1)S(1)} %pad_maximum_fusion.refs_1_), channel_id=1, source_target_pairs={{0,1},{1,0},{2,3},{3,2},{4,5},{5,4},{6,7},{7,6},{8,9},{9,8},{10,11... | collective-permute-start | bytes 1769480 | tf_op jit(solution)/shard_map/ppermute | solution.py:93
  63.5 14.5 %collective-permute-start.18 = (bf16[2,9,32,256]{3,2,1,0:T(8,128)(2,1)S(1)}, bf16[2,9,32,256]{3,2,1,0:T(8,128)(2,1)S(1)}, u32[]{:S(2)}, u32[]{:S(2)}) collective-permute-start(bf16[2,9,32,256]{3,2,1,0:T(8,128)(2,1)S(1)} %slice.14), channel_id=1, source_target_pairs={{0,2},{2,0},{4,6},{6,4},{8,10},{10,8},{12,14},{14,12},{16,18},{18,... | collective-permute-start | bytes 884744 | tf_op jit(solution)/shard_map/ppermute | solution.py:89
  66.5 11.5 %collective-permute-start.19 = (bf16[2,9,32,256]{3,2,1,0:T(8,128)(2,1)S(1)}, bf16[2,9,32,256]{3,2,1,0:T(8,128)(2,1)S(1)}, u32[]{:S(2)}, u32[]{:S(2)}) collective-permute-start(bf16[2,9,32,256]{3,2,1,0:T(8,128)(2,1)S(1)} %slice.15), channel_id=1, source_target_pairs={{0,4},{2,6},{4,0},{6,2},{8,12},{10,14},{12,8},{14,10},{16,20},{18,... | collective-permute-start | bytes 884744 | tf_op jit(solution)/shard_map/ppermute | solution.py:89
  69.9 10.1 %collective-permute-start.21 = (bf16[4,9,32,256]{3,2,1,0:T(8,128)(2,1)S(1)}, bf16[4,9,32,256]{3,2,1,0:T(8,128)(2,1)S(1)}, u32[]{:S(2)}, u32[]{:S(2)}) collective-permute-start(bf16[4,9,32,256]{3,2,1,0:T(8,128)(2,1)S(1)} %collective-permute-done.16.refs_2_), channel_id=1, source_target_pairs={{0,1},{1,0},{2,3},{3,2},{4,5},{5,4},{6,7},{7,6},{8,9},{9,8},{10,11... | collective-permute-start | bytes 1769480 | tf_op jit(solution)/shard_map/ppermute | solution.py:93
  75.7 4.3 %collective-permute-start.22 = (bf16[4,9,32,256]{3,2,1,0:T(8,128)(2,1)S(1)}, bf16[4,9,32,256]{3,2,1,0:T(8,128)(2,1)S(1)}, u32[]{:S(2)}, u32[]{:S(2)}) collective-permute-start(bf16[4,9,32,256]{3,2,1,0:T(8,128)(2,1)S(1)} %collective-permute-done.17.refs_3_), channel_id=1, source_target_pairs={{0,1},{1,0},{2,3},{3,2},{4,5},{5,4},{6,7},{7,6},{8,9},{9,8},{10,11... | collective-permute-start | bytes 1769480 | tf_op jit(solution)/shard_map/ppermute | solution.py:93
  78.0 1.6 %collective-permute-start.23 = (bf16[2,9,32,256]{3,2,1,0:T(8,128)(2,1)S(1)}, bf16[2,9,32,256]{3,2,1,0:T(8,128)(2,1)S(1)}, u32[]{:S(2)}, u32[]{:S(2)}) collective-permute-start(bf16[2,9,32,256]{3,2,1,0:T(8,128)(2,1)S(1)} %collective-permute-done.18.refs_4_), channel_id=1, source_target_pairs={{0,1},{1,0},{2,3},{3,2},{4,5},{5,4},{6,7},{7,6},{8,9},{9,8},{10,11... | collective-permute-start | bytes 884744 | tf_op jit(solution)/shard_map/ppermute | solution.py:93
  78.0 2.0 %collective-permute-start.24 = (bf16[2,9,32,256]{3,2,1,0:T(8,128)(2,1)S(1)}, bf16[2,9,32,256]{3,2,1,0:T(8,128)(2,1)S(1)}, u32[]{:S(2)}, u32[]{:S(2)}) collective-permute-start(bf16[2,9,32,256]{3,2,1,0:T(8,128)(2,1)S(1)} %collective-permute-done.19.refs_5_), channel_id=1, source_target_pairs={{0,1},{1,0},{2,3},{3,2},{4,5},{5,4},{6,7},{7,6},{8,9},{9,8},{10,11... | collective-permute-start | bytes 884744 | tf_op jit(solution)/shard_map/ppermute | solution.py:93

commit v2 on v1

--- a/solution.py
+++ b/solution.py
@@ -10,7 +10,7 @@
 TAPS = (((1, 1), (3, 0)), ((2, 1), (0, 2)))
 FRAME_COST = 0
 PACK_COST = 0
-SPLIT = 12
+SPLIT = 8
 VMEM_LIMIT = 16 * 1024 * 1024
 X, Y, Z0, Z1 = 1, 2, 4, 8
 
@@ -356,12 +356,12 @@
         tuple(m ^ X ^ Y for m in order[2:]),
     )
     others = [swap_cores(block) for block in mine]
-    hops = (0, X, Z1, X | Z1)
+    hops = (0, X, X | Z1, Z1)
     pieces = [
         near_same,
         exchange(near_across, X),
+        exchange(far_across, X | Z1),
         exchange(far_same, Z1),
-        exchange(far_across, X | Z1),
     ]
     (framed,) = local_call(
         functools.partial(frame_body, (batch, hops)),

time: 84.9 us -> 82.9 us (0.976)
  starting transfers between devices: 30 us -> 25.8 us
  waiting for transfers between devices: 37.6 us -> 39.8 us
    ppermute x17, starting transfers between devices: 27.6 us -> 23.7 us  [exchange(): lax.ppermute(block, 'lon', [(i, i ^ bits) for i in range(lax.axis_size('l...]
    ppermute x17, waiting for transfers between devices: 36.9 us -> 39.1 us  [exchange(): lax.ppermute(block, 'lon', [(i, i ^ bits) for i in range(lax.axis_size('l...]
  transfers between devices with their start and end apart: 25 -> 25, of which waited for: 11 -> 12; matrix products, arithmetic and copies ran while one was open for 4% -> 4% of each run, Pallas kernels for 10% -> 10%
where the time goes in v2:
time: 82.9 us; the launch traced here: 82.7 us
  waiting for transfers between devices  39.8 us (48%)
  starting transfers between devices  25.8 us (31%)
  Pallas kernels  13.3 us (16%)
  local copies, waits for them, and re-layouts  3.25 us (4%)
    ppermute x17, waiting for transfers between devices, exchange(): lax.ppermute(block, 'lon', [(i, i ^ bits) for i in range(lax.axis_size('l...  39.1 us
    ppermute x17, starting transfers between devices, exchange(): lax.ppermute(block, 'lon', [(i, i ^ bits) for i in range(lax.axis_size('l...  23.7 us
    pallas_call x7, Pallas kernels, local_call(): pl.pallas_call(body, out_shape=outs, in_specs=specs, out_specs=[pl.BlockS...  13.3 us
    ppermute x2, starting transfers between devices, grouped_shards(): lax.ppermute(edge, 'lon', [(i, (i + (step if i % 2 else -step)) % lon) fo...  1.78 us
  transfers between devices with their start and end apart: 25, of which 12 were waited for; matrix products, arithmetic and copies ran while one was open for 4% of the time, Pallas kernels for 10%

profile of v2, /device:TPU:0, one launch (start us, length us, event | category | flops | bytes accessed | tf_op | source)
XLA Modules:
  0.0 82.7 jit_solution(6765323009965111779)
XLA Ops:
  0.0 3.0 %collective-permute-start.2 = (bf16[16,32,512]{2,1,0:T(8,128)(2,1)}, bf16[16,32,512]{2,1,0:T(8,128)(2,1)S(1)}, u32[]{:S(2)}, u32[]{:S(2)}) collective-permute-start(bf16[16,32,512]{2,1,0:T(8,128)(2,1)} %bitcast.16), channel_id=1, source_target_pairs={{0,4},{2,6},{4,0},{6,2},{8,12},{10,14},{12,8},{14,10},{16,20},{18,... | collective-permute-start | bytes 1572872 | tf_op jit(solution)/shard_map/ppermute | solution.py:89
  3.0 1.6 %collective-permute-start.3 = (bf16[16,32,512]{2,1,0:T(8,128)(2,1)}, bf16[16,32,512]{2,1,0:T(8,128)(2,1)S(1)}, u32[]{:S(2)}, u32[]{:S(2)}) collective-permute-start(bf16[16,32,512]{2,1,0:T(8,128)(2,1)} %bitcast.17), channel_id=1, source_target_pairs={{0,8},{2,10},{4,12},{6,14},{8,0},{10,2},{12,4},{14,6},{16,24},{18,... | collective-permute-start | bytes 1572872 | tf_op jit(solution)/shard_map/ppermute | solution.py:89
  4.5 1.1 %copy.9 = bf16[16,4,4,512]{3,2,1,0:T(4,128)(2,1)S(1)} copy(bf16[16,4,4,512]{3,1,2,0:T(4,128)(2,1)} %bitcast.23) | data formatting | bytes 524288 | tf_op jit(solution)/shard_map/transpose | solution.py:287
  5.7 2.7 %collective-permute-start = (bf16[16,16,512]{2,1,0:T(8,128)(2,1)S(1)}, bf16[16,16,512]{2,1,0:T(8,128)(2,1)S(1)}, u32[]{:S(2)}, u32[]{:S(2)}) collective-permute-start(bf16[16,16,512]{2,1,0:T(8,128)(2,1)S(1)} %reshape.23.refs_2_), channel_id=1, source_target_pairs={{0,16},{2,18},{4,20},{6,22},{8,24},{10,26},{12,28},{14,30},{16,0},... | collective-permute-start | bytes 786440 | tf_op jit(solution)/shard_map/ppermute | solution.py:89
  8.4 1.5 %collective-permute-start.1 = (bf16[16,16,512]{2,1,0:T(8,128)(2,1)S(1)}, bf16[16,16,512]{2,1,0:T(8,128)(2,1)S(1)}, u32[]{:S(2)}, u32[]{:S(2)}) collective-permute-start(bf16[16,16,512]{2,1,0:T(8,128)(2,1)S(1)} %reshape.23.refs_2_), channel_id=1, source_target_pairs={{0,2},{2,0},{4,6},{6,4},{8,10},{10,8},{12,14},{14,12},{16,18},{18,... | collective-permute-start | bytes 786440 | tf_op jit(solution)/shard_map/ppermute | solution.py:89
  9.8 1.1 %constant_dynamic-slice_fusion.1 = bf16[16,4,1,512]{3,2,1,0:T(2,128)(2,1)S(1)} fusion(bf16[16,4,4,512]{3,2,1,0:T(4,128)(2,1)} %param.5, s32[]{:T(128)S(6)} %select_n.35), kind=kLoop, calls=%fused_computation.5 | loop fusion | bytes 131076 | tf_op jit(solution)/shard_map/dynamic_slice | solution.py:280
  11.1 0.8 reshape.25
  12.0 10.0 %collective-permute-done.refs_0_ = bf16[16,16,512]{2,1,0:T(8,128)(2,1)S(1)} collective-permute-done((bf16[16,16,512]{2,1,0:T(8,128)(2,1)S(1)}, bf16[16,16,512]{2,1,0:T(8,128)(2,1)S(1)}, u32[]{:S(2)}, u32[]{:S(2)}) %collective-permute-start) | collective-permute-done | bytes 262176 | tf_op jit(solution)/shard_map/ppermute | solution.py:89
  22.0 1.7 %collective-permute-start.6 = (bf16[16,4,1,512]{3,1,0,2:T(4,128)(2,1)S(1)}, bf16[16,4,1,512]{3,1,0,2:T(4,128)(2,1)S(1)}, u32[]{:S(2)}, u32[]{:S(2)}) collective-permute-start(bf16[16,4,1,512]{3,1,0,2:T(4,128)(2,1)S(1)} %copy.11), channel_id=1, source_target_pairs={{0,28},{2,6},{4,0},{6,10},{8,4},{10,14},{12,8},{14,18},{16,12},{18... | collective-permute-start | bytes 196616 | tf_op jit(solution)/shard_map/ppermute | solution.py:282
  23.8 2.5 %collective-permute-start.14 = (bf16[9,32,256]{2,1,0:T(8,128)(2,1)S(1)}, bf16[9,32,256]{2,1,0:T(8,128)(2,1)S(1)}, u32[]{:S(2)}, u32[]{:S(2)}) collective-permute-start(bf16[9,32,256]{2,1,0:T(8,128)(2,1)S(1)} %constant_dynamic-slice_fusion), channel_id=1, source_target_pairs={{0,16},{2,18},{4,20},{6,22},{8,24},{10,26},{12,28},{14,30},{16,0},... | collective-permute-start | bytes 442376 | tf_op jit(solution)/shard_map/ppermute | solution.py:89
  26.3 1.3 %collective-permute-start.8 = (bf16[8,32,512]{2,1,0:T(8,128)(2,1)S(1)}, bf16[8,32,512]{2,1,0:T(8,128)(2,1)S(1)}, u32[]{:S(2)}, u32[]{:S(2)}) collective-permute-start(bf16[8,32,512]{2,1,0:T(8,128)(2,1)S(1)} %slice.12), channel_id=1, source_target_pairs={{0,4},{2,6},{4,0},{6,2},{8,12},{10,14},{12,8},{14,10},{16,20},{18,... | collective-permute-start | bytes 786440 | tf_op jit(solution)/shard_map/ppermute | solution.py:89
  27.8 1.1 %collective-permute-start.4 = (bf16[16,16,512]{2,1,0:T(8,128)(2,1)S(1)}, bf16[16,16,512]{2,1,0:T(8,128)(2,1)S(1)}, u32[]{:S(2)}, u32[]{:S(2)}) collective-permute-start(bf16[16,16,512]{2,1,0:T(8,128)(2,1)S(1)} %collective-permute-done.refs_0_), channel_id=1, source_target_pairs={{0,2},{2,0},{4,6},{6,4},{8,10},{10,8},{12,14},{14,12},{16,18},{18,... | collective-permute-start | bytes 786440 | tf_op jit(solution)/shard_map/ppermute | solution.py:89
  29.0 2.5 %collective-permute-start.7 = (bf16[2,16,4,512]{3,2,1,0:T(4,128)(2,1)S(1)}, bf16[2,16,4,512]{3,2,1,0:T(4,128)(2,1)S(1)}, u32[]{:S(2)}, u32[]{:S(2)}) collective-permute-start(bf16[2,16,4,512]{3,2,1,0:T(4,128)(2,1)S(1)} %pad_maximum_fusion.2.refs_5_), channel_id=1, source_target_pairs={{0,16},{2,18},{4,20},{6,22},{8,24},{10,26},{12,28},{14,30},{16,0},... | collective-permute-start | bytes 393224 | tf_op jit(solution)/shard_map/ppermute | solution.py:89
  31.6 3.5 %collective-permute-done.14 = bf16[9,32,256]{2,1,0:T(8,128)(2,1)S(1)} collective-permute-done((bf16[9,32,256]{2,1,0:T(8,128)(2,1)S(1)}, bf16[9,32,256]{2,1,0:T(8,128)(2,1)S(1)}, u32[]{:S(2)}, u32[]{:S(2)}) %collective-permute-start.14) | collective-permute-done | bytes 147488 | tf_op jit(solution)/shard_map/ppermute | solution.py:89
  35.2 0.7 shard_map.55.begun
  35.8 5.0 %collective-permute-done.9.second = bf16[8,32,512]{2,1,0:T(8,128)(2,1)S(1)} collective-permute-done((bf16[8,32,512]{2,1,0:T(8,128)(2,1)S(1)}, bf16[8,32,512]{2,1,0:T(8,128)(2,1)S(1)}, u32[]{:S(2)}, u32[]{:S(2)}) %collective-permute-start.9) | collective-permute-done | bytes 262176 | tf_op jit(solution)/shard_map/ppermute | solution.py:89
  40.9 0.6 shard_map.56.refs_6_
  41.5 2.7 %shard_map.57 = bf16[2,9,40,512]{3,2,1,0:T(8,128)(2,1)S(1)} custom-call(s32[2]{0:T(128)S(1)} %pad_add_fusion.place, bf16[16,16,512]{2,1,0:T(8,128)(2,1)S(1)} %collective-permute-done.refs_0_, bf16[16,16,512]{2,1,0:T(8,128)(2,1)S(1)} %collective-permute-done.4.refs_1_, bf16[16,16,512]{2,1,0:T(8,128)(2,1)S(1)} %reshape.23.refs_2_, ...), custom_call_target="tpu_custom_call" | custom-call | flops 1509949440 | bytes 8388608 | tf_op jit(solution)/shard_map/pallas_call | solution.py:253
  44.3 0.9 %collective-permute-done.15 = bf16[2,9,32,256]{3,2,1,0:T(8,128)(2,1)S(1)} collective-permute-done((bf16[2,9,32,256]{3,2,1,0:T(8,128)(2,1)S(1)}, bf16[2,9,32,256]{3,2,1,0:T(8,128)(2,1)S(1)}, u32[]{:S(2)}, u32[]{:S(2)}) %collective-permute-start.15) | collective-permute-done | bytes 294944 | tf_op jit(solution)/shard_map/ppermute | solution.py:89
  45.3 2.8 %collective-permute-start.17 = (bf16[4,9,32,256]{3,2,1,0:T(8,128)(2,1)S(1)}, bf16[4,9,32,256]{3,2,1,0:T(8,128)(2,1)S(1)}, u32[]{:S(2)}, u32[]{:S(2)}) collective-permute-start(bf16[4,9,32,256]{3,2,1,0:T(8,128)(2,1)S(1)} %pad_maximum_fusion.refs_1_), channel_id=1, source_target_pairs={{0,4},{2,6},{4,0},{6,2},{8,12},{10,14},{12,8},{14,10},{16,20},{18,... | collective-permute-start | bytes 1769480 | tf_op jit(solution)/shard_map/ppermute | solution.py:89
  48.1 2.7 %shard_map.58.refs_0_ = bf16[2,9,40,512]{3,2,1,0:T(8,128)(2,1)S(1)} custom-call(s32[2]{0:T(128)S(1)} %pad_add_fusion.place, bf16[16,16,512]{2,1,0:T(8,128)(2,1)S(1)} %collective-permute-done.refs_0_, bf16[16,16,512]{2,1,0:T(8,128)(2,1)S(1)} %collective-permute-done.4.refs_1_, bf16[16,16,512]{2,1,0:T(8,128)(2,1)S(1)} %reshape.23.refs_2_, ...), custom_call_target="tpu_custom_call" | custom-call | flops 1509949440 | bytes 8388608 | tf_op jit(solution)/shard_map/pallas_call | solution.py:253
  50.8 1.2 %shard_map.59 = (bf16[9,20,512]{2,1,0:T(8,128)(2,1)S(1)}, bf16[9,20,512]{2,1,0:T(8,128)(2,1)S(1)}, bf16[9,20,512]{2,1,0:T(8,128)(2,1)S(1)}, bf16[9,20,512]{2,1,0:T(8,128)(2,1)S(1)}) custom-call(s32[2]{0:T(128)S(1)} %pad_add_fusion.place, bf16[2,9,40,512]{3,2,1,0:T(8,128)(2,1)S(1)} %shard_map.58.refs_0_, ...), custom_call_target="tpu_custom_call" | custom-call | flops 14745600 | bytes 8388608 | tf_op jit(solution)/shard_map/pallas_call | solution.py:253
  52.2 2.2 %collective-permute-start.12 = (bf16[9,20,512]{2,1,0:T(8,128)(2,1)S(1)}, bf16[9,20,512]{2,1,0:T(8,128)(2,1)S(1)}, u32[]{:S(2)}, u32[]{:S(2)}) collective-permute-start(bf16[9,20,512]{2,1,0:T(8,128)(2,1)S(1)} %get-tuple-element.27), channel_id=1, source_target_pairs={{0,18},{2,16},{4,22},{6,20},{8,26},{10,24},{12,30},{14,28},{16,2},... | collective-permute-start | bytes 552968 | tf_op jit(solution)/shard_map/ppermute | solution.py:89
  54.3 2.1 %collective-permute-start.13 = (bf16[9,20,512]{2,1,0:T(8,128)(2,1)S(1)}, bf16[9,20,512]{2,1,0:T(8,128)(2,1)S(1)}, u32[]{:S(2)}, u32[]{:S(2)}) collective-permute-start(bf16[9,20,512]{2,1,0:T(8,128)(2,1)S(1)} %get-tuple-element.28), channel_id=1, source_target_pairs={{0,16},{2,18},{4,20},{6,22},{8,24},{10,26},{12,28},{14,30},{16,0},... | collective-permute-start | bytes 552968 | tf_op jit(solution)/shard_map/ppermute | solution.py:89
  56.5 6.3 %collective-permute-done.16.refs_2_ = bf16[4,9,32,256]{3,2,1,0:T(8,128)(2,1)S(1)} collective-permute-done((bf16[4,9,32,256]{3,2,1,0:T(8,128)(2,1)S(1)}, bf16[4,9,32,256]{3,2,1,0:T(8,128)(2,1)S(1)}, u32[]{:S(2)}, u32[]{:S(2)}) %collective-permute-start.16) | collective-permute-done | bytes 589856 | tf_op jit(solution)/shard_map/ppermute | solution.py:89
  62.9 6.7 %collective-permute-done.11.refs_1_ = bf16[9,20,512]{2,1,0:T(8,128)(2,1)S(1)} collective-permute-done((bf16[9,20,512]{2,1,0:T(8,128)(2,1)S(1)}, bf16[9,20,512]{2,1,0:T(8,128)(2,1)S(1)}, u32[]{:S(2)}, u32[]{:S(2)}) %collective-permute-start.11) | collective-permute-done | bytes 184352 | tf_op jit(solution)/shard_map/ppermute | solution.py:89
  69.6 0.8 collective-permute-done.12.refs_2_
  70.4 3.7 %collective-permute-done.13.refs_3_ = bf16[9,20,512]{2,1,0:T(8,128)(2,1)S(1)} collective-permute-done((bf16[9,20,512]{2,1,0:T(8,128)(2,1)S(1)}, bf16[9,20,512]{2,1,0:T(8,128)(2,1)S(1)}, u32[]{:S(2)}, u32[]{:S(2)}) %collective-permute-start.13) | collective-permute-done | bytes 184352 | tf_op jit(solution)/shard_map/ppermute | solution.py:89
  74.1 1.8 %collective-permute-done.18.refs_4_ = bf16[2,9,32,256]{3,2,1,0:T(8,128)(2,1)S(1)} collective-permute-done((bf16[2,9,32,256]{3,2,1,0:T(8,128)(2,1)S(1)}, bf16[2,9,32,256]{3,2,1,0:T(8,128)(2,1)S(1)}, u32[]{:S(2)}, u32[]{:S(2)}) %collective-permute-start.18) | collective-permute-done | bytes 294944 | tf_op jit(solution)/shard_map/ppermute | solution.py:89
  76.5 0.8 shard_map.60.refs_0_
  77.5 0.4 collective-permute-done.24.refs_10_
  78.0 4.7 %shard_map.61 = bf16[16,4,8,512]{3,2,1,0:T(8,128)(2,1)} custom-call(s32[2]{0:T(128)S(1)} %pad_add_fusion.place, bf16[18,4,16,512]{3,2,1,0:T(8,128)(2,1)S(1)} %shard_map.60.refs_0_, bf16[4,9,32,256]{3,2,1,0:T(8,128)(2,1)S(1)} %pad_maximum_fusion.refs_1_, bf16[4,9,32,256]{3,2,1,0:T(8,128)(2,1)S(1)} %collective-permute-done.16.refs_2_, ...), custom_call_target="tpu_custom_call" | custom-call | flops 2415919104 | bytes 8388608 | tf_op jit(solution)/shard_map/pallas_call | solution.py:253
  (49 shorter events, 2.1 us)
Async XLA Ops:
  0.0 12.0 %copy-start = (bf16[3,3,32,512]{3,2,1,0:T(8,128)(2,1)S(1)}, bf16[3,3,32,512]{3,2,1,0:T(8,128)(2,1)}, u32[]{:S(2)}) copy-start(bf16[3,3,32,512]{3,2,1,0:T(8,128)(2,1)} %param.8) | copy-start | bytes 884740
  0.0 35.1 %copy-start.1 = (bf16[4,4,512,32]{2,3,1,0:T(8,128)(2,1)S(1)}, bf16[4,4,512,32]{2,3,1,0:T(8,128)(2,1)}, u32[]{:S(2)}) copy-start(bf16[4,4,512,32]{2,3,1,0:T(8,128)(2,1)} %param.6) | copy-start | bytes 1572868
  0.0 26.3 %collective-permute-start.2 = (bf16[16,32,512]{2,1,0:T(8,128)(2,1)}, bf16[16,32,512]{2,1,0:T(8,128)(2,1)S(1)}, u32[]{:S(2)}, u32[]{:S(2)}) collective-permute-start(bf16[16,32,512]{2,1,0:T(8,128)(2,1)} %bitcast.16), channel_id=1, source_target_pairs={{0,4},{2,6},{4,0},{6,2},{8,12},{10,14},{12,8},{14,10},{16,20},{18,... | collective-permute-start | bytes 1572872 | tf_op jit(solution)/shard_map/ppermute | solution.py:89
  3.0 23.3 %collective-permute-start.3 = (bf16[16,32,512]{2,1,0:T(8,128)(2,1)}, bf16[16,32,512]{2,1,0:T(8,128)(2,1)S(1)}, u32[]{:S(2)}, u32[]{:S(2)}) collective-permute-start(bf16[16,32,512]{2,1,0:T(8,128)(2,1)} %bitcast.17), channel_id=1, source_target_pairs={{0,8},{2,10},{4,12},{6,14},{8,0},{10,2},{12,4},{14,6},{16,24},{18,... | collective-permute-start | bytes 1572872 | tf_op jit(solution)/shard_map/ppermute | solution.py:89
  5.7 16.3 %collective-permute-start = (bf16[16,16,512]{2,1,0:T(8,128)(2,1)S(1)}, bf16[16,16,512]{2,1,0:T(8,128)(2,1)S(1)}, u32[]{:S(2)}, u32[]{:S(2)}) collective-permute-start(bf16[16,16,512]{2,1,0:T(8,128)(2,1)S(1)} %reshape.23.refs_2_), channel_id=1, source_target_pairs={{0,16},{2,18},{4,20},{6,22},{8,24},{10,26},{12,28},{14,30},{16,0},... | collective-permute-start | bytes 786440 | tf_op jit(solution)/shard_map/ppermute | solution.py:89
  8.4 15.4 %collective-permute-start.1 = (bf16[16,16,512]{2,1,0:T(8,128)(2,1)S(1)}, bf16[16,16,512]{2,1,0:T(8,128)(2,1)S(1)}, u32[]{:S(2)}, u32[]{:S(2)}) collective-permute-start(bf16[16,16,512]{2,1,0:T(8,128)(2,1)S(1)} %reshape.23.refs_2_), channel_id=1, source_target_pairs={{0,2},{2,0},{4,6},{6,4},{8,10},{10,8},{12,14},{14,12},{16,18},{18,... | collective-permute-start | bytes 786440 | tf_op jit(solution)/shard_map/ppermute | solution.py:89
  11.0 16.8 %collective-permute-start.5 = (bf16[16,4,1,512]{3,1,0,2:T(4,128)(2,1)S(1)}, bf16[16,4,1,512]{3,1,0,2:T(4,128)(2,1)S(1)}, u32[]{:S(2)}, u32[]{:S(2)}) collective-permute-start(bf16[16,4,1,512]{3,1,0,2:T(4,128)(2,1)S(1)} %copy.11), channel_id=1, source_target_pairs={{0,30},{2,4},{4,2},{6,8},{8,6},{10,12},{12,10},{14,16},{16,14},{18... | collective-permute-start | bytes 196616 | tf_op jit(solution)/shard_map/ppermute | solution.py:282
  22.0 6.9 %collective-permute-start.6 = (bf16[16,4,1,512]{3,1,0,2:T(4,128)(2,1)S(1)}, bf16[16,4,1,512]{3,1,0,2:T(4,128)(2,1)S(1)}, u32[]{:S(2)}, u32[]{:S(2)}) collective-permute-start(bf16[16,4,1,512]{3,1,0,2:T(4,128)(2,1)S(1)} %copy.11), channel_id=1, source_target_pairs={{0,28},{2,6},{4,0},{6,10},{8,4},{10,14},{12,8},{14,18},{16,12},{18... | collective-permute-start | bytes 196616 | tf_op jit(solution)/shard_map/ppermute | solution.py:282
  23.8 11.3 %collective-permute-start.14 = (bf16[9,32,256]{2,1,0:T(8,128)(2,1)S(1)}, bf16[9,32,256]{2,1,0:T(8,128)(2,1)S(1)}, u32[]{:S(2)}, u32[]{:S(2)}) collective-permute-start(bf16[9,32,256]{2,1,0:T(8,128)(2,1)S(1)} %constant_dynamic-slice_fusion), channel_id=1, source_target_pairs={{0,16},{2,18},{4,20},{6,22},{8,24},{10,26},{12,28},{14,30},{16,0},... | collective-permute-start | bytes 442376 | tf_op jit(solution)/shard_map/ppermute | solution.py:89
  26.3 9.5 %collective-permute-start.8 = (bf16[8,32,512]{2,1,0:T(8,128)(2,1)S(1)}, bf16[8,32,512]{2,1,0:T(8,128)(2,1)S(1)}, u32[]{:S(2)}, u32[]{:S(2)}) collective-permute-start(bf16[8,32,512]{2,1,0:T(8,128)(2,1)S(1)} %slice.12), channel_id=1, source_target_pairs={{0,4},{2,6},{4,0},{6,2},{8,12},{10,14},{12,8},{14,10},{16,20},{18,... | collective-permute-start | bytes 786440 | tf_op jit(solution)/shard_map/ppermute | solution.py:89
  27.6 13.3 %collective-permute-start.9 = (bf16[8,32,512]{2,1,0:T(8,128)(2,1)S(1)}, bf16[8,32,512]{2,1,0:T(8,128)(2,1)S(1)}, u32[]{:S(2)}, u32[]{:S(2)}) collective-permute-start(bf16[8,32,512]{2,1,0:T(8,128)(2,1)S(1)} %slice.13), channel_id=1, source_target_pairs={{0,8},{2,10},{4,12},{6,14},{8,0},{10,2},{12,4},{14,6},{16,24},{18,... | collective-permute-start | bytes 786440 | tf_op jit(solution)/shard_map/ppermute | solution.py:89
  27.8 13.7 %collective-permute-start.4 = (bf16[16,16,512]{2,1,0:T(8,128)(2,1)S(1)}, bf16[16,16,512]{2,1,0:T(8,128)(2,1)S(1)}, u32[]{:S(2)}, u32[]{:S(2)}) collective-permute-start(bf16[16,16,512]{2,1,0:T(8,128)(2,1)S(1)} %collective-permute-done.refs_0_), channel_id=1, source_target_pairs={{0,2},{2,0},{4,6},{6,4},{8,10},{10,8},{12,14},{14,12},{16,18},{18,... | collective-permute-start | bytes 786440 | tf_op jit(solution)/shard_map/ppermute | solution.py:89
  29.0 12.5 %collective-permute-start.7 = (bf16[2,16,4,512]{3,2,1,0:T(4,128)(2,1)S(1)}, bf16[2,16,4,512]{3,2,1,0:T(4,128)(2,1)S(1)}, u32[]{:S(2)}, u32[]{:S(2)}) collective-permute-start(bf16[2,16,4,512]{3,2,1,0:T(4,128)(2,1)S(1)} %pad_maximum_fusion.2.refs_5_), channel_id=1, source_target_pairs={{0,16},{2,18},{4,20},{6,22},{8,24},{10,26},{12,28},{14,30},{16,0},... | collective-permute-start | bytes 393224 | tf_op jit(solution)/shard_map/ppermute | solution.py:89
  35.1 10.1 %collective-permute-start.15 = (bf16[2,9,32,256]{3,2,1,0:T(8,128)(2,1)S(1)}, bf16[2,9,32,256]{3,2,1,0:T(8,128)(2,1)S(1)}, u32[]{:S(2)}, u32[]{:S(2)}) collective-permute-start(bf16[2,9,32,256]{3,2,1,0:T(8,128)(2,1)S(1)} %pad_maximum_fusion.1), channel_id=1, source_target_pairs={{0,8},{2,10},{4,12},{6,14},{8,0},{10,2},{12,4},{14,6},{16,24},{18,... | collective-permute-start | bytes 884744 | tf_op jit(solution)/shard_map/ppermute | solution.py:89
  44.2 6.6 %collective-permute-start.10 = (bf16[2,9,40,512]{3,2,1,0:T(8,128)(2,1)S(1)}, bf16[2,9,40,512]{3,2,1,0:T(8,128)(2,1)S(1)}, u32[]{:S(2)}, u32[]{:S(2)}) collective-permute-start(bf16[2,9,40,512]{3,2,1,0:T(8,128)(2,1)S(1)} %shard_map.57), channel_id=1, source_target_pairs={{0,1},{1,0},{2,3},{3,2},{4,5},{5,4},{6,7},{7,6},{8,9},{9,8},{10,11... | collective-permute-start | bytes 2211848 | tf_op jit(solution)/shard_map/ppermute | solution.py:93
  45.2 17.5 %collective-permute-start.16 = (bf16[4,9,32,256]{3,2,1,0:T(8,128)(2,1)S(1)}, bf16[4,9,32,256]{3,2,1,0:T(8,128)(2,1)S(1)}, u32[]{:S(2)}, u32[]{:S(2)}) collective-permute-start(bf16[4,9,32,256]{3,2,1,0:T(8,128)(2,1)S(1)} %pad_maximum_fusion.refs_1_), channel_id=1, source_target_pairs={{0,2},{2,0},{4,6},{6,4},{8,10},{10,8},{12,14},{14,12},{16,18},{18,... | collective-permute-start | bytes 1769480 | tf_op jit(solution)/shard_map/ppermute | solution.py:89
  45.3 17.4 %collective-permute-start.17 = (bf16[4,9,32,256]{3,2,1,0:T(8,128)(2,1)S(1)}, bf16[4,9,32,256]{3,2,1,0:T(8,128)(2,1)S(1)}, u32[]{:S(2)}, u32[]{:S(2)}) collective-permute-start(bf16[4,9,32,256]{3,2,1,0:T(8,128)(2,1)S(1)} %pad_maximum_fusion.refs_1_), channel_id=1, source_target_pairs={{0,4},{2,6},{4,0},{6,2},{8,12},{10,14},{12,8},{14,10},{16,20},{18,... | collective-permute-start | bytes 1769480 | tf_op jit(solution)/shard_map/ppermute | solution.py:89
  50.8 27.2 %copy-start.2 = (f32[512]{0:T(512)S(1)}, f32[512]{0:T(512)}, u32[]{:S(2)}) copy-start(f32[512]{0:T(512)} %param.9) | copy-start | bytes 6148
  52.0 17.6 %collective-permute-start.11 = (bf16[9,20,512]{2,1,0:T(8,128)(2,1)S(1)}, bf16[9,20,512]{2,1,0:T(8,128)(2,1)S(1)}, u32[]{:S(2)}, u32[]{:S(2)}) collective-permute-start(bf16[9,20,512]{2,1,0:T(8,128)(2,1)S(1)} %get-tuple-element.26), channel_id=1, source_target_pairs={{0,2},{2,0},{4,6},{6,4},{8,10},{10,8},{12,14},{14,12},{16,18},{18,... | collective-permute-start | bytes 552968 | tf_op jit(solution)/shard_map/ppermute | solution.py:89
  52.2 18.2 %collective-permute-start.12 = (bf16[9,20,512]{2,1,0:T(8,128)(2,1)S(1)}, bf16[9,20,512]{2,1,0:T(8,128)(2,1)S(1)}, u32[]{:S(2)}, u32[]{:S(2)}) collective-permute-start(bf16[9,20,512]{2,1,0:T(8,128)(2,1)S(1)} %get-tuple-element.27), channel_id=1, source_target_pairs={{0,18},{2,16},{4,22},{6,20},{8,26},{10,24},{12,30},{14,28},{16,2},... | collective-permute-start | bytes 552968 | tf_op jit(solution)/shard_map/ppermute | solution.py:89
  54.3 19.8 %collective-permute-start.13 = (bf16[9,20,512]{2,1,0:T(8,128)(2,1)S(1)}, bf16[9,20,512]{2,1,0:T(8,128)(2,1)S(1)}, u32[]{:S(2)}, u32[]{:S(2)}) collective-permute-start(bf16[9,20,512]{2,1,0:T(8,128)(2,1)S(1)} %get-tuple-element.28), channel_id=1, source_target_pairs={{0,16},{2,18},{4,20},{6,22},{8,24},{10,26},{12,28},{14,30},{16,0},... | collective-permute-start | bytes 552968 | tf_op jit(solution)/shard_map/ppermute | solution.py:89
  62.7 14.6 %collective-permute-start.20 = (bf16[4,9,32,256]{3,2,1,0:T(8,128)(2,1)S(1)}, bf16[4,9,32,256]{3,2,1,0:T(8,128)(2,1)S(1)}, u32[]{:S(2)}, u32[]{:S(2)}) collective-permute-start(bf16[4,9,32,256]{3,2,1,0:T(8,128)(2,1)S(1)} %pad_maximum_fusion.refs_1_), channel_id=1, source_target_pairs={{0,1},{1,0},{2,3},{3,2},{4,5},{5,4},{6,7},{7,6},{8,9},{9,8},{10,11... | collective-permute-start | bytes 1769480 | tf_op jit(solution)/shard_map/ppermute | solution.py:93
  62.7 13.2 %collective-permute-start.18 = (bf16[2,9,32,256]{3,2,1,0:T(8,128)(2,1)S(1)}, bf16[2,9,32,256]{3,2,1,0:T(8,128)(2,1)S(1)}, u32[]{:S(2)}, u32[]{:S(2)}) collective-permute-start(bf16[2,9,32,256]{3,2,1,0:T(8,128)(2,1)S(1)} %slice.14), channel_id=1, source_target_pairs={{0,2},{2,0},{4,6},{6,4},{8,10},{10,8},{12,14},{14,12},{16,18},{18,... | collective-permute-start | bytes 884744 | tf_op jit(solution)/shard_map/ppermute | solution.py:89
  69.6 6.7 %collective-permute-start.19 = (bf16[2,9,32,256]{3,2,1,0:T(8,128)(2,1)S(1)}, bf16[2,9,32,256]{3,2,1,0:T(8,128)(2,1)S(1)}, u32[]{:S(2)}, u32[]{:S(2)}) collective-permute-start(bf16[2,9,32,256]{3,2,1,0:T(8,128)(2,1)S(1)} %slice.15), channel_id=1, source_target_pairs={{0,4},{2,6},{4,0},{6,2},{8,12},{10,14},{12,8},{14,10},{16,20},{18,... | collective-permute-start | bytes 884744 | tf_op jit(solution)/shard_map/ppermute | solution.py:89
  70.4 7.6 %collective-permute-start.21 = (bf16[4,9,32,256]{3,2,1,0:T(8,128)(2,1)S(1)}, bf16[4,9,32,256]{3,2,1,0:T(8,128)(2,1)S(1)}, u32[]{:S(2)}, u32[]{:S(2)}) collective-permute-start(bf16[4,9,32,256]{3,2,1,0:T(8,128)(2,1)S(1)} %collective-permute-done.16.refs_2_), channel_id=1, source_target_pairs={{0,1},{1,0},{2,3},{3,2},{4,5},{5,4},{6,7},{7,6},{8,9},{9,8},{10,11... | collective-permute-start | bytes 1769480 | tf_op jit(solution)/shard_map/ppermute | solution.py:93
  74.1 3.9 %collective-permute-start.22 = (bf16[4,9,32,256]{3,2,1,0:T(8,128)(2,1)S(1)}, bf16[4,9,32,256]{3,2,1,0:T(8,128)(2,1)S(1)}, u32[]{:S(2)}, u32[]{:S(2)}) collective-permute-start(bf16[4,9,32,256]{3,2,1,0:T(8,128)(2,1)S(1)} %collective-permute-done.17.refs_3_), channel_id=1, source_target_pairs={{0,1},{1,0},{2,3},{3,2},{4,5},{5,4},{6,7},{7,6},{8,9},{9,8},{10,11... | collective-permute-start | bytes 1769480 | tf_op jit(solution)/shard_map/ppermute | solution.py:93
  76.0 1.6 %collective-permute-start.23 = (bf16[2,9,32,256]{3,2,1,0:T(8,128)(2,1)S(1)}, bf16[2,9,32,256]{3,2,1,0:T(8,128)(2,1)S(1)}, u32[]{:S(2)}, u32[]{:S(2)}) collective-permute-start(bf16[2,9,32,256]{3,2,1,0:T(8,128)(2,1)S(1)} %collective-permute-done.18.refs_4_), channel_id=1, source_target_pairs={{0,1},{1,0},{2,3},{3,2},{4,5},{5,4},{6,7},{7,6},{8,9},{9,8},{10,11... | collective-permute-start | bytes 884744 | tf_op jit(solution)/shard_map/ppermute | solution.py:93
  76.3 1.7 %collective-permute-start.24 = (bf16[2,9,32,256]{3,2,1,0:T(8,128)(2,1)S(1)}, bf16[2,9,32,256]{3,2,1,0:T(8,128)(2,1)S(1)}, u32[]{:S(2)}, u32[]{:S(2)}) collective-permute-start(bf16[2,9,32,256]{3,2,1,0:T(8,128)(2,1)S(1)} %collective-permute-done.19.refs_5_), channel_id=1, source_target_pairs={{0,1},{1,0},{2,3},{3,2},{4,5},{5,4},{6,7},{7,6},{8,9},{9,8},{10,11... | collective-permute-start | bytes 884744 | tf_op jit(solution)/shard_map/ppermute | solution.py:93
